TPU v7x, 256 devices: a whole 4x4x8 slice. The times are simulated.
256 devices in a mesh: blk: 64 (over z, x, core), grp: 4 (over y).
Axes of the slice: x: 4, y: 4, z: 8, core: 2. Of those that a mesh axis runs over, the one named last changes fastest.
Arguments:
- embeddings: bfloat16 [768, 1024, 1024], P(('blk', 'grp'))
- ranks: int32 [768, 1024], P(('blk', 'grp')), may hold values from 0 to 1048575
- block_rows: int32 [768], P(('blk', 'grp')), may hold values from 1 to 1024, as said below
- pair_list: int32 [256, 6, 2], P(('blk', 'grp')), may hold values from 1 to 5, as said below
- pair_count: int32 [256], P(('blk', 'grp')), may hold values from 1 to 6, as said below
Outputs:
- best: float32 [768, 1024], P(('blk', 'grp'))
Inputs may be any that keep to these rules, and one draw needn't show every extreme that they name: `block_rows`: A block that is not the last of its cluster has 1024 live rows. `pair_list`: the blocks fall into clusters of 1 to 3 consecutive blocks, some of exactly 3. The first pair_count entries of a device are (u, v) with 3 <= u < 6 and u - 3 < v <= u, naming two blocks of one cluster or a block with itself; over all devices they name every such pair of a cluster once, at the device of the later block; the other entries are (3, 3). `pair_count`: some device has 6 live slots.
All inputs are finite; a program needn't handle non-finite values.
Results may differ from a plain program's by a relative error of at most 0.0003.
Values may be sent and summed in bfloat16 or wider, within the bound.
No kernel may reach another device: no remote copies, remote signals or barrier semaphores. Data moves between devices by JAX's collectives and lax.ppermute only.
A program may use at most 128 MiB of HBM per device.

v0:
```python
import functools

import jax
import jax.numpy as jnp
from jax import lax
from jax.experimental import pallas as pl
from jax.experimental.pallas import tpu as pltpu
from jax.sharding import PartitionSpec as P

ROWS = 1024
DIM = 1024
HELD = 3
COLS = 256
LANES = 128
NOTE = 16
CUTS = (0, 512, 896, 1024)
DIGIT = 128
DEAD = DIGIT**3 - 1
NONE = -1e30
AXES = ("blk", "grp")
SMEM = pl.BlockSpec(memory_space=pltpu.SMEM)
VMEM = pl.BlockSpec(memory_space=pltpu.VMEM)
HBM = pl.BlockSpec(memory_space=pltpu.HBM)


def exchanged(value, first):
    count = lax.axis_size(AXES)
    pairs = [(low, low + 1) for low in range(first, count - 1, 2)]
    return lax.ppermute(value, AXES, pairs + [(high, low) for low, high in pairs])


def odd_device():
    return lax.axis_index(AXES[-1]) % 2


def shaped(shape, dtype):
    return jax.ShapeDtypeStruct(shape, dtype)


def unit_rows(raw):
    values = raw.astype(jnp.float32)
    scaling = lax.rsqrt(jnp.sum(values * values, axis=-1, keepdims=True) + 1e-06)
    return (values * scaling).astype(jnp.bfloat16)


def normalize(raw, units, rows):
    def step(index, carry):
        at = pl.ds(pl.multiple_of(index * LANES, LANES), LANES)
        units[at, :] = unit_rows(raw[at, :])
        return carry

    lax.fori_loop(0, rows // LANES, step, 0, unroll=2 if rows % (2 * LANES) == 0 else True)


def spread(keys_row):
    return jnp.broadcast_to(keys_row, (LANES, LANES)).T


def gathered(partial):
    return jnp.max(partial.T, axis=0, keepdims=True)


def shifted(found):
    return jnp.maximum(1.0 + found, 0.0)


def pair_tile(left_units, left_keys, right_units, right_keys):
    similarity = lax.dot_general(
        left_units, right_units, (((1,), (1,)), ((), ())), preferred_element_type=jnp.float32
    )
    rows, cols = similarity.shape
    left_best = None
    right_best = []
    for group in range(cols // LANES):
        part = similarity[:, group * LANES : (group + 1) * LANES]
        keys = right_keys[:, group * LANES : (group + 1) * LANES]
        for_left = jnp.where(keys < left_keys, part, NONE)
        left_best = for_left if left_best is None else jnp.maximum(left_best, for_left)
        for_right = jnp.where(left_keys < keys, part, NONE)
        right_best.append(jnp.max(for_right.reshape(rows // 8, 8, LANES), axis=0))
    return left_best, jnp.concatenate(right_best, axis=1)


def pair_strip(first, left_units, left_keys, left_acc, right_units, right_keys, right_acc, cols):
    rows = pl.ds(first, left_units.shape[0] - first)
    left_best, right_best = pair_tile(left_units[rows, :], left_keys[rows, :], right_units[cols, :], right_keys[:, cols])
    left_acc[rows, :] = jnp.maximum(left_acc[rows, :], left_best)
    right_acc[:, cols] = jnp.maximum(right_acc[:, cols], right_best)


def note_rows(keys, flags):
    row = lax.broadcasted_iota(jnp.int32, (NOTE, ROWS), 0)
    values = [keys % DIGIT, (keys // DIGIT) % DIGIT, keys // DIGIT**2] + flags
    note = jnp.zeros((NOTE, ROWS), jnp.int32)
    for index, value in enumerate(values):
        note = jnp.where(row == index, value, note)
    return note.astype(jnp.float32).astype(jnp.bfloat16)


def noted_keys(note):
    digits = note.astype(jnp.float32).astype(jnp.int32)
    return digits[0:1] + digits[1:2] * DIGIT + digits[2:3] * DIGIT**2


def piece_copies(index, odd, raw, to_even, to_odd, sems):
    first, rows = CUTS[index], CUTS[index + 1] - CUTS[index]
    last_block = HELD - 1
    return [
        pltpu.make_async_copy(raw.at[block, pl.ds(first, rows)], piece.at[pl.ds(0, rows)], sems.at[index, side])
        for side, (block, piece) in enumerate(((last_block * (1 - odd), to_even), (last_block * odd, to_odd)))
    ]


def first_kernel(
    pairs_hbm, live_hbm, ranks_hbm, raw, even_on, odd_on, keys, flags,
    pairs, live, ranks, sems, small_sems,
):
    odd = odd_device()
    copies = piece_copies(0, odd, raw, even_on, odd_on, sems)
    small = [
        pltpu.make_async_copy(source, target, small_sems.at[index])
        for index, (source, target) in enumerate(((pairs_hbm, pairs), (live_hbm, live), (ranks_hbm, ranks)))
    ]
    for copy in small + copies:
        copy.start()
    for copy in small:
        copy.wait()
    position = lax.broadcasted_iota(jnp.int32, (1, ROWS), 1)
    for block in range(HELD):
        keys[block : block + 1, :] = jnp.where(position < live[block], ranks[block : block + 1, :], DEAD)

    def listed(u, v):
        found = jnp.int32(0)
        for slot in range(pairs.shape[2]):
            found = found | ((pairs[0, 0, slot] == u) & (pairs[0, 1, slot] == v)).astype(jnp.int32)
        return found

    ahead, near, far = listed(HELD + 1, HELD - 1), listed(HELD, HELD - 1), listed(HELD, HELD - 2)
    flags[0] = ahead * near
    flags[1] = ahead
    note_last = note_rows(keys[HELD - 1 : HELD, :], [])
    note_first = note_rows(keys[0:1, :], [(1 - ahead) * near, far])
    even_on[pl.ds(CUTS[1], NOTE), :] = jnp.where(odd == 1, note_first, note_last)
    odd_on[pl.ds(CUTS[1], NOTE), :] = jnp.where(odd == 1, note_last, note_first)
    for copy in copies:
        copy.wait()


def in_hbm(*values):
    return [pltpu.with_memory_space_constraint(value, pltpu.HBM) for value in values]


def first_pieces(pairs, live, ranks, raw):
    piece = shaped((CUTS[1] + NOTE, DIM), jnp.bfloat16)
    return pl.pallas_call(
        first_kernel,
        out_shape=(piece, piece, shaped((HELD, ROWS), jnp.int32), shaped((2,), jnp.int32)),
        in_specs=[HBM] * 4,
        out_specs=(VMEM,) * 3 + (SMEM,),
        scratch_shapes=[
            pltpu.SMEM(pairs.shape, jnp.int32),
            pltpu.SMEM(live.shape, jnp.int32),
            pltpu.VMEM(ranks.shape, jnp.int32),
            pltpu.SemaphoreType.DMA((2, 2)),
            pltpu.SemaphoreType.DMA((3,)),
        ],
        compiler_params=pltpu.CompilerParams(vmem_limit_bytes=6 << 20),
        cost_estimate=pl.CostEstimate(flops=0, bytes_accessed=8 * CUTS[1] * DIM, transcendentals=0),
    )(*in_hbm(pairs, live, ranks, raw))


def local_kernel(pairs, count, raw, keys, units, best, even_on, odd_on, spread_keys, left_acc, right_acc, sems):
    copies = piece_copies(1, odd_device(), raw, even_on, odd_on, sems)
    for copy in copies:
        copy.start()
    for block in range(HELD):
        for group in range(ROWS // LANES):
            rows = pl.ds(group * LANES, LANES)
            spread_keys[block, rows, :] = spread(keys[block : block + 1, rows])
        normalize(raw.at[block], units.at[block], ROWS)
    left_acc[...] = jnp.full_like(left_acc, NONE)
    right_acc[...] = jnp.full_like(right_acc, NONE)

    def visit(slot, carry):
        left, right = pairs[0, 0, slot] - HELD, pairs[0, 1, slot] - HELD

        def strip(first, col):
            pair_strip(
                first, units.at[left], spread_keys.at[left], left_acc.at[left],
                units.at[right], keys.at[pl.ds(right, 1)], right_acc.at[right], pl.ds(col, COLS),
            )

        @pl.when(right == left)
        def _():
            for col in range(0, ROWS, COLS):
                strip(col, col)

        @pl.when((right >= 0) & (right != left))
        def _():
            for col in range(0, ROWS, COLS):
                strip(0, col)

        return carry

    lax.fori_loop(0, count[0], visit, 0)
    for block in range(HELD):
        for group in range(ROWS // LANES):
            rows = pl.ds(group * LANES, LANES)
            found = jnp.maximum(
                gathered(left_acc[block, rows, :]),
                jnp.max(right_acc[block, :, rows], axis=0, keepdims=True),
            )
            best[block : block + 1, rows] = shifted(found)
    for copy in copies:
        copy.wait()


def local_pairs(pairs, count, raw, keys):
    piece = shaped((CUTS[2] - CUTS[1], DIM), jnp.bfloat16)
    return pl.pallas_call(
        local_kernel,
        out_shape=(shaped((HELD, ROWS, DIM), jnp.bfloat16), shaped((HELD, ROWS), jnp.float32), piece, piece),
        in_specs=[SMEM, SMEM, VMEM, VMEM],
        out_specs=(VMEM,) * 4,
        scratch_shapes=[
            pltpu.VMEM((HELD, ROWS, LANES), jnp.int32),
            pltpu.VMEM((HELD, ROWS, LANES), jnp.float32),
            pltpu.VMEM((HELD, 8, ROWS), jnp.float32),
            pltpu.SemaphoreType.DMA((3, 2)),
        ],
        compiler_params=pltpu.CompilerParams(vmem_limit_bytes=24 << 20),
        cost_estimate=pl.CostEstimate(flops=6 * 2 * ROWS * ROWS * DIM, bytes_accessed=4 * HELD * ROWS * DIM, transcendentals=0),
    )(pairs, count, raw, keys)


def last_kernel(raw, after, even_on, odd_on, sems):
    copies = piece_copies(2, odd_device(), raw, even_on, odd_on, sems)
    for copy in copies:
        copy.start()
    for copy in copies:
        copy.wait()


def last_pieces(raw, after):
    piece = shaped((CUTS[3] - CUTS[2], DIM), jnp.bfloat16)
    return pl.pallas_call(
        last_kernel,
        out_shape=(piece, piece),
        in_specs=[HBM, pl.BlockSpec(memory_space=pl.ANY)],
        out_specs=(VMEM, VMEM),
        scratch_shapes=[pltpu.SemaphoreType.DMA((3, 2))],
        compiler_params=pltpu.CompilerParams(vmem_limit_bytes=2 << 20),
        cost_estimate=pl.CostEstimate(flops=0, bytes_accessed=8 * (CUTS[3] - CUTS[2]) * DIM, transcendentals=0),
    )(*in_hbm(raw), after)


def guest_pairs(flags, after, raw, rows, guest_keys, keys, units, right_acc, guest_units, spread_keys, left_acc):
    cols = max(COLS, min(ROWS, COLS * ROWS // rows // COLS * COLS))
    left_acc[...] = jnp.full_like(left_acc, NONE)
    some_live = jnp.min(guest_keys[:, :LANES].astype(jnp.float32)) < DEAD

    @pl.when(((flags[0] != 0) | (flags[1] != 0)) & some_live)
    def _():
        normalize(raw, guest_units, rows)
        for group in range(rows // LANES):
            at = pl.ds(group * LANES, LANES)
            spread_keys[at, :] = spread(guest_keys[:, group * LANES : (group + 1) * LANES])

        def visit(which, carry):
            block = which + after * (HELD - 1 - 2 * which)

            @pl.when(flags[which] != 0)
            def _():
                for col in range(0, ROWS, cols):
                    pair_strip(
                        0, guest_units, spread_keys, left_acc,
                        units.at[block], keys.at[pl.ds(block, 1)], right_acc.at[block], pl.ds(col, cols),
                    )

            return carry

        lax.fori_loop(0, 2, visit, 0)


def finish_guests(left_acc, first, guest_earlier, guest_best):
    if first:
        guest_best[:, pl.ds(0, first)] = guest_earlier[...]
    for group in range(left_acc.shape[0] // LANES):
        found = gathered(left_acc[pl.ds(group * LANES, LANES), :])
        guest_best[:, pl.ds(first + group * LANES, LANES)] = shifted(found)


def finish_held(right_acc, best_before, best):
    for block in range(HELD):
        found = jnp.max(right_acc[block], axis=0, keepdims=True)
        best[block : block + 1, :] = jnp.maximum(best_before[block : block + 1, :], shifted(found))


def guest_scratch(rows):
    return [
        pltpu.VMEM((HELD, 8, ROWS), jnp.float32),
        pltpu.VMEM((rows, DIM), jnp.bfloat16),
        pltpu.VMEM((rows, LANES), jnp.int32),
        pltpu.VMEM((rows, LANES), jnp.float32),
    ]


def guest_cost(rows, blocks):
    return pl.CostEstimate(flops=2 * blocks * rows * ROWS * DIM, bytes_accessed=2 * (rows + HELD * ROWS) * DIM, transcendentals=0)


def first_guests_kernel(
    flags, even_raw, odd_raw, keys, units, best_before,
    even_guest, odd_guest, best, even_keys, odd_keys, even_flags, odd_flags, right_acc, *scratch,
):
    odd = odd_device()
    rows = CUTS[1]
    right_acc[...] = jnp.full_like(right_acc, NONE)
    sides = (
        (1 - odd, even_raw, even_keys, even_flags, even_guest),
        (odd, odd_raw, odd_keys, odd_flags, odd_guest),
    )
    for after, guest_raw, guest_keys, guest_flags, guest_best in sides:
        note = guest_raw[pl.ds(rows, NOTE), :]
        guest_keys[...] = noted_keys(note)
        for which in range(2):
            noted = (jnp.max(note[3 + which : 4 + which, :].astype(jnp.float32)) > 0.5).astype(jnp.int32)
            guest_flags[which] = jnp.where(after == 1, noted, flags[which])
        guest_pairs(guest_flags, after, guest_raw, rows, guest_keys[:, :rows], keys, units, right_acc, *scratch)
        finish_guests(scratch[-1], 0, None, guest_best)
    finish_held(right_acc, best_before, best)


def first_guests(flags, even_raw, odd_raw, keys, units, best_before):
    row = shaped((1, ROWS), jnp.int32)
    two = shaped((2,), jnp.int32)
    guest = shaped((1, CUTS[1]), jnp.float32)
    return pl.pallas_call(
        first_guests_kernel,
        out_shape=(guest, guest, shaped((HELD, ROWS), jnp.float32), row, row, two, two),
        in_specs=[SMEM] + [VMEM] * 5,
        out_specs=(VMEM,) * 5 + (SMEM,) * 2,
        scratch_shapes=guest_scratch(CUTS[1]),
        compiler_params=pltpu.CompilerParams(vmem_limit_bytes=16 << 20),
        cost_estimate=guest_cost(CUTS[1], 3),
    )(flags, even_raw, odd_raw, keys, units, best_before)


def next_guests_kernel(
    index, even_flags, odd_flags, even_raw, odd_raw, even_keys, odd_keys, keys, units, even_earlier, odd_earlier, best_before,
    even_guest, odd_guest, best, right_acc, *scratch,
):
    first, last = CUTS[index], CUTS[index + 1]
    odd = odd_device()
    right_acc[...] = jnp.full_like(right_acc, NONE)
    sides = (
        (1 - odd, even_raw, even_keys, even_flags, even_earlier, even_guest),
        (odd, odd_raw, odd_keys, odd_flags, odd_earlier, odd_guest),
    )
    for after, guest_raw, guest_keys, guest_flags, guest_earlier, guest_best in sides:
        guest_pairs(guest_flags, after, guest_raw, last - first, guest_keys[:, first:last], keys, units, right_acc, *scratch)
        finish_guests(scratch[-1], first, guest_earlier, guest_best)
    finish_held(right_acc, best_before, best)


def next_guests(index, even_flags, odd_flags, even_raw, odd_raw, even_keys, odd_keys, keys, units, *earlier):
    guest = shaped((1, CUTS[index + 1]), jnp.float32)
    rows = CUTS[index + 1] - CUTS[index]
    return pl.pallas_call(
        functools.partial(next_guests_kernel, index),
        out_shape=(guest, guest, shaped((HELD, ROWS), jnp.float32)),
        in_specs=[SMEM, SMEM] + [VMEM] * 9,
        out_specs=(VMEM,) * 3,
        scratch_shapes=guest_scratch(rows),
        compiler_params=pltpu.CompilerParams(vmem_limit_bytes=16 << 20),
        cost_estimate=guest_cost(rows, 3),
    )(even_flags, odd_flags, even_raw, odd_raw, even_keys, odd_keys, keys, units, *earlier)


def combined_kernel(keys, best_before, even_found, odd_found, best):
    odd = odd_device() == 1
    even, other = even_found[...], odd_found[...]
    found = (jnp.where(odd, even, other), jnp.zeros_like(even), jnp.where(odd, other, even))
    for block in range(HELD):
        rows = slice(block, block + 1)
        best[rows, :] = jnp.where(keys[rows, :] != DEAD, jnp.maximum(best_before[rows, :], found[block]), 0.0)


def combined(keys, best, even_found, odd_found):
    return pl.pallas_call(
        combined_kernel,
        out_shape=shaped((HELD, ROWS), jnp.float32),
        in_specs=[VMEM] * 4,
        out_specs=VMEM,
        compiler_params=pltpu.CompilerParams(vmem_limit_bytes=2 << 20),
        cost_estimate=pl.CostEstimate(flops=0, bytes_accessed=8 * HELD * ROWS, transcendentals=0),
    )(keys, best, even_found, odd_found)


def local(embeddings, ranks, block_rows, pair_list, pair_count):
    pairs = pair_list.transpose(0, 2, 1)
    even_on, odd_on, keys, flags = first_pieces(pairs, block_rows, ranks, embeddings)
    even_first, odd_first = exchanged(even_on, 0), exchanged(odd_on, 1)
    units, best, even_on, odd_on = local_pairs(pairs, pair_count, embeddings, keys)
    even_next, odd_next = exchanged(even_on, 0), exchanged(odd_on, 1)
    even_on, odd_on = last_pieces(embeddings, best)
    even_last, odd_last = exchanged(even_on, 0), exchanged(odd_on, 1)
    even_guest, odd_guest, best, even_keys, odd_keys, even_flags, odd_flags = first_guests(
        flags, even_first, odd_first, keys, units, best
    )
    known = (even_keys, odd_keys, keys, units)
    guests = next_guests(1, even_flags, odd_flags, even_next, odd_next, *known, even_guest, odd_guest, best)
    even_guest, odd_guest, best = next_guests(2, even_flags, odd_flags, even_last, odd_last, *known, *guests)
    even_found, odd_found = exchanged(even_guest, 0), exchanged(odd_guest, 1)
    return combined(keys, best, even_found, odd_found)


def solution(mesh):
    in_specs = (
        P(AXES, None, None),
        P(AXES, None),
        P(AXES),
        P(AXES, None, None),
        P(AXES),
    )
    return jax.shard_map(local, mesh=mesh, in_specs=in_specs, out_specs=P(AXES, None), check_vma=False)
```

profile of v0, /device:TPU:161, one launch (start us, length us, event | category | flops | bytes accessed | tf_op | source)
XLA Modules:
  0.0 68.6 jit_solution(17571897517649301384)
XLA Ops:
  0.0 0.0 copy-start
  0.0 0.0 copy-start.1
  0.0 2.4 %shard_map.55 = (bf16[528,1024]{1,0:T(8,128)(2,1)S(1)}, bf16[528,1024]{1,0:T(8,128)(2,1)S(1)}, s32[3,1024]{1,0:T(4,128)S(1)}, s32[2]{0:T(128)S(1)}) custom-call(s32[1,2,6]{2,1,0:T(2,128)} %bitcast.1, s32[3]{0:T(128)} %live_hbm.1, s32[3,1024]{1,0:T(4,128)} %ranks_hbm.1, bf16[3,1024,1024]{2,1,0:T(8,128)(2,1)} %raw.5), custom_call_target="tpu_custom_call" | custom-call | bytes 4194304 | tf_op jit(solution)/shard_map/pallas_call | solution.py:155
  2.4 1.4 %collective-permute-start = (bf16[528,1024]{1,0:T(8,128)(2,1)S(1)}, bf16[528,1024]{1,0:T(8,128)(2,1)S(1)}, u32[]{:S(2)}, u32[]{:S(2)}) collective-permute-start(bf16[528,1024]{1,0:T(8,128)(2,1)S(1)} %get-tuple-element.30), channel_id=1, source_target_pairs={{0,1},{2,3},{4,5},{6,7},{8,9},{10,11},{12,13},{14,15},{16,17},{18,... | collective-permute-start | bytes 3244040 | tf_op jit(solution)/shard_map/ppermute | solution.py:29
  3.8 4.6 %collective-permute-start.1 = (bf16[528,1024]{1,0:T(8,128)(2,1)S(1)}, bf16[528,1024]{1,0:T(8,128)(2,1)S(1)}, u32[]{:S(2)}, u32[]{:S(2)}) collective-permute-start(bf16[528,1024]{1,0:T(8,128)(2,1)S(1)} %get-tuple-element.31), channel_id=1, source_target_pairs={{1,2},{3,4},{5,6},{7,8},{9,10},{11,12},{13,14},{15,16},{17,18},{19... | collective-permute-start | bytes 3244040 | tf_op jit(solution)/shard_map/ppermute | solution.py:29
  9.1 0.0 copy-done
  9.1 0.0 copy-done.1
  9.1 12.0 %shard_map.56 = (bf16[3,1024,1024]{2,1,0:T(8,128)(2,1)S(1)}, f32[3,1024]{1,0:T(4,128)S(1)}, bf16[384,1024]{1,0:T(8,128)(2,1)S(1)}, bf16[384,1024]{1,0:T(8,128)(2,1)S(1)}) custom-call(s32[1,2,6]{2,1,0:T(2,128)S(1)} %bitcast.2, s32[1]{0:T(128)S(6)} %copy.6.count, bf16[3,1024,1024]{2,1,0:T(8,128)(2,1)S(1)} %copy-done, s32[3,1024]{1,0:T(4,128)S(1)} %get-tuple-element.28.keys), custom_call_target="tpu_custom_call" | custom-call | flops 12884901888 | bytes 12582912 | tf_op jit(solution)/shard_map/pallas_call | solution.py:220
  21.0 5.2 %collective-permute-start.4 = (bf16[384,1024]{1,0:T(8,128)(2,1)S(1)}, bf16[384,1024]{1,0:T(8,128)(2,1)S(1)}, u32[]{:S(2)}, u32[]{:S(2)}) collective-permute-start(bf16[384,1024]{1,0:T(8,128)(2,1)S(1)} %get-tuple-element.40), channel_id=1, source_target_pairs={{0,1},{2,3},{4,5},{6,7},{8,9},{10,11},{12,13},{14,15},{16,17},{18,... | collective-permute-start | bytes 2359304 | tf_op jit(solution)/shard_map/ppermute | solution.py:29
  26.2 1.9 %collective-permute-start.5 = (bf16[384,1024]{1,0:T(8,128)(2,1)S(1)}, bf16[384,1024]{1,0:T(8,128)(2,1)S(1)}, u32[]{:S(2)}, u32[]{:S(2)}) collective-permute-start(bf16[384,1024]{1,0:T(8,128)(2,1)S(1)} %get-tuple-element.41), channel_id=1, source_target_pairs={{1,2},{3,4},{5,6},{7,8},{9,10},{11,12},{13,14},{15,16},{17,18},{19... | collective-permute-start | bytes 2359304 | tf_op jit(solution)/shard_map/ppermute | solution.py:29
  28.1 1.1 %shard_map.58 = (bf16[128,1024]{1,0:T(8,128)(2,1)S(1)}, bf16[128,1024]{1,0:T(8,128)(2,1)S(1)}) custom-call(bf16[3,1024,1024]{2,1,0:T(8,128)(2,1)} %raw.5, f32[3,1024]{1,0:T(4,128)S(1)} %get-tuple-element.33.best_before.after), custom_call_target="tpu_custom_call" | custom-call | bytes 1048576 | tf_op jit(solution)/shard_map/pallas_call | solution.py:246
  29.2 0.1 collective-permute-start.2
  29.3 0.0 collective-permute-done.even_raw
  29.3 8.8 %collective-permute-start.3 = (bf16[128,1024]{1,0:T(8,128)(2,1)S(1)}, bf16[128,1024]{1,0:T(8,128)(2,1)S(1)}, u32[]{:S(2)}, u32[]{:S(2)}) collective-permute-start(bf16[128,1024]{1,0:T(8,128)(2,1)S(1)} %get-tuple-element.37), channel_id=1, source_target_pairs={{1,2},{3,4},{5,6},{7,8},{9,10},{11,12},{13,14},{15,16},{17,18},{19... | collective-permute-start | bytes 786440 | tf_op jit(solution)/shard_map/ppermute | solution.py:29
  38.1 5.2 %collective-permute-done.1.odd_raw = bf16[528,1024]{1,0:T(8,128)(2,1)S(1)} collective-permute-done((bf16[528,1024]{1,0:T(8,128)(2,1)S(1)}, bf16[528,1024]{1,0:T(8,128)(2,1)S(1)}, u32[]{:S(2)}, u32[]{:S(2)}) %collective-permute-start.1) | collective-permute-done | bytes 1081376 | tf_op jit(solution)/shard_map/ppermute | solution.py:29
  43.3 1.5 %shard_map.57 = (f32[1,512]{1,0:T(1,128)S(1)}, f32[1,512]{1,0:T(1,128)S(1)}, f32[3,1024]{1,0:T(4,128)S(1)}, s32[1,1024]{1,0:T(1,128)S(1)}, s32[1,1024]{1,0:T(1,128)S(1)}, /*index=5*/s32[2]{0:T(128)S(1)}, s32[2]{0:T(128)S(1)}) custom-call(s32[2]{0:T(128)S(1)} %get-tuple-element.29.flags, bf16[528,1024]{1,0:T(8,128)(2,1)S(1)} %collective-permute-done.even_raw, ...), custom_call_target="tpu_custom_call" | custom-call | flops 3221225472 | bytes 7340032 | tf_op jit(solution)/shard_map/pallas_call | solution.py:338
  44.8 0.0 collective-permute-done.4.even_raw
  44.8 7.9 %collective-permute-done.5.odd_raw = bf16[384,1024]{1,0:T(8,128)(2,1)S(1)} collective-permute-done((bf16[384,1024]{1,0:T(8,128)(2,1)S(1)}, bf16[384,1024]{1,0:T(8,128)(2,1)S(1)}, u32[]{:S(2)}, u32[]{:S(2)}) %collective-permute-start.5) | collective-permute-done | bytes 786464 | tf_op jit(solution)/shard_map/ppermute | solution.py:29
  52.7 1.1 %shard_map.59 = (f32[1,896]{1,0:T(1,128)S(1)}, f32[1,896]{1,0:T(1,128)S(1)}, f32[3,1024]{1,0:T(4,128)S(1)}) custom-call(s32[2]{0:T(128)S(1)} %get-tuple-element.34.even_flags, s32[2]{0:T(128)S(1)} %get-tuple-element.35.odd_flags, bf16[384,1024]{1,0:T(8,128)(2,1)S(1)} %collective-permute-done.4.even_raw, ...), custom_call_target="tpu_custom_call" | custom-call | flops 2415919104 | bytes 7077888 | tf_op jit(solution)/shard_map/pallas_call | solution.py:369
  53.8 0.0 collective-permute-done.2.even_raw
  53.8 1.7 %collective-permute-done.3.odd_raw = bf16[128,1024]{1,0:T(8,128)(2,1)S(1)} collective-permute-done((bf16[128,1024]{1,0:T(8,128)(2,1)S(1)}, bf16[128,1024]{1,0:T(8,128)(2,1)S(1)}, u32[]{:S(2)}, u32[]{:S(2)}) %collective-permute-start.3) | collective-permute-done | bytes 262176 | tf_op jit(solution)/shard_map/ppermute | solution.py:29
  55.5 0.9 %shard_map.60 = (f32[1,1024]{1,0:T(1,128)S(1)}, f32[1,1024]{1,0:T(1,128)S(1)}, f32[3,1024]{1,0:T(4,128)S(1)}) custom-call(s32[2]{0:T(128)S(1)} %get-tuple-element.34.even_flags, s32[2]{0:T(128)S(1)} %get-tuple-element.35.odd_flags, bf16[128,1024]{1,0:T(8,128)(2,1)S(1)} %collective-permute-done.2.even_raw, ...), custom_call_target="tpu_custom_call" | custom-call | flops 805306368 | bytes 6553600 | tf_op jit(solution)/shard_map/pallas_call | solution.py:369
  56.4 0.1 collective-permute-start.6
  56.5 10.2 %collective-permute-start.7 = (f32[1,1024]{1,0:T(1,128)S(1)}, f32[1,1024]{1,0:T(1,128)S(1)}, u32[]{:S(2)}, u32[]{:S(2)}) collective-permute-start(f32[1,1024]{1,0:T(1,128)S(1)} %get-tuple-element.50), channel_id=1, source_target_pairs={{1,2},{3,4},{5,6},{7,8},{9,10},{11,12},{13,14},{15,16},{17,18},{19... | collective-permute-start | bytes 12296 | tf_op jit(solution)/shard_map/ppermute | solution.py:29
  66.7 0.0 collective-permute-done.6.even_found
  66.7 1.3 %collective-permute-done.7.odd_found = f32[1,1024]{1,0:T(1,128)S(1)} collective-permute-done((f32[1,1024]{1,0:T(1,128)S(1)}, f32[1,1024]{1,0:T(1,128)S(1)}, u32[]{:S(2)}, u32[]{:S(2)}) %collective-permute-start.7) | collective-permute-done | bytes 4128 | tf_op jit(solution)/shard_map/ppermute | solution.py:29
  68.0 0.6 shard_map.61
Async XLA Ops:
  0.0 9.1 %copy-start = (bf16[3,1024,1024]{2,1,0:T(8,128)(2,1)S(1)}, bf16[3,1024,1024]{2,1,0:T(8,128)(2,1)}, u32[]{:S(2)}) copy-start(bf16[3,1024,1024]{2,1,0:T(8,128)(2,1)} %raw.5) | copy-start | bytes 18874372
  0.0 9.1 %copy-start.1 = (s32[1,6,2]{1,2,0:T(2,128)S(1)}, s32[1,6,2]{1,2,0:T(2,128)}, u32[]{:S(2)}) copy-start(s32[1,6,2]{1,2,0:T(2,128)} %param.8) | copy-start | bytes 148
  2.4 27.0 %collective-permute-start = (bf16[528,1024]{1,0:T(8,128)(2,1)S(1)}, bf16[528,1024]{1,0:T(8,128)(2,1)S(1)}, u32[]{:S(2)}, u32[]{:S(2)}) collective-permute-start(bf16[528,1024]{1,0:T(8,128)(2,1)S(1)} %get-tuple-element.30), channel_id=1, source_target_pairs={{0,1},{2,3},{4,5},{6,7},{8,9},{10,11},{12,13},{14,15},{16,17},{18,... | collective-permute-start | bytes 3244040 | tf_op jit(solution)/shard_map/ppermute | solution.py:29
  3.8 39.5 %collective-permute-start.1 = (bf16[528,1024]{1,0:T(8,128)(2,1)S(1)}, bf16[528,1024]{1,0:T(8,128)(2,1)S(1)}, u32[]{:S(2)}, u32[]{:S(2)}) collective-permute-start(bf16[528,1024]{1,0:T(8,128)(2,1)S(1)} %get-tuple-element.31), channel_id=1, source_target_pairs={{1,2},{3,4},{5,6},{7,8},{9,10},{11,12},{13,14},{15,16},{17,18},{19... | collective-permute-start | bytes 3244040 | tf_op jit(solution)/shard_map/ppermute | solution.py:29
  21.0 23.8 %collective-permute-start.4 = (bf16[384,1024]{1,0:T(8,128)(2,1)S(1)}, bf16[384,1024]{1,0:T(8,128)(2,1)S(1)}, u32[]{:S(2)}, u32[]{:S(2)}) collective-permute-start(bf16[384,1024]{1,0:T(8,128)(2,1)S(1)} %get-tuple-element.40), channel_id=1, source_target_pairs={{0,1},{2,3},{4,5},{6,7},{8,9},{10,11},{12,13},{14,15},{16,17},{18,... | collective-permute-start | bytes 2359304 | tf_op jit(solution)/shard_map/ppermute | solution.py:29
  26.2 26.5 %collective-permute-start.5 = (bf16[384,1024]{1,0:T(8,128)(2,1)S(1)}, bf16[384,1024]{1,0:T(8,128)(2,1)S(1)}, u32[]{:S(2)}, u32[]{:S(2)}) collective-permute-start(bf16[384,1024]{1,0:T(8,128)(2,1)S(1)} %get-tuple-element.41), channel_id=1, source_target_pairs={{1,2},{3,4},{5,6},{7,8},{9,10},{11,12},{13,14},{15,16},{17,18},{19... | collective-permute-start | bytes 2359304 | tf_op jit(solution)/shard_map/ppermute | solution.py:29
  29.2 24.6 %collective-permute-start.2 = (bf16[128,1024]{1,0:T(8,128)(2,1)S(1)}, bf16[128,1024]{1,0:T(8,128)(2,1)S(1)}, u32[]{:S(2)}, u32[]{:S(2)}) collective-permute-start(bf16[128,1024]{1,0:T(8,128)(2,1)S(1)} %get-tuple-element.36), channel_id=1, source_target_pairs={{0,1},{2,3},{4,5},{6,7},{8,9},{10,11},{12,13},{14,15},{16,17},{18,... | collective-permute-start | bytes 786440 | tf_op jit(solution)/shard_map/ppermute | solution.py:29
  29.3 26.1 %collective-permute-start.3 = (bf16[128,1024]{1,0:T(8,128)(2,1)S(1)}, bf16[128,1024]{1,0:T(8,128)(2,1)S(1)}, u32[]{:S(2)}, u32[]{:S(2)}) collective-permute-start(bf16[128,1024]{1,0:T(8,128)(2,1)S(1)} %get-tuple-element.37), channel_id=1, source_target_pairs={{1,2},{3,4},{5,6},{7,8},{9,10},{11,12},{13,14},{15,16},{17,18},{19... | collective-permute-start | bytes 786440 | tf_op jit(solution)/shard_map/ppermute | solution.py:29
  56.4 10.3 %collective-permute-start.6 = (f32[1,1024]{1,0:T(1,128)S(1)}, f32[1,1024]{1,0:T(1,128)S(1)}, u32[]{:S(2)}, u32[]{:S(2)}) collective-permute-start(f32[1,1024]{1,0:T(1,128)S(1)} %get-tuple-element.49), channel_id=1, source_target_pairs={{0,1},{2,3},{4,5},{6,7},{8,9},{10,11},{12,13},{14,15},{16,17},{18,... | collective-permute-start | bytes 12296 | tf_op jit(solution)/shard_map/ppermute | solution.py:29
  56.5 11.5 %collective-permute-start.7 = (f32[1,1024]{1,0:T(1,128)S(1)}, f32[1,1024]{1,0:T(1,128)S(1)}, u32[]{:S(2)}, u32[]{:S(2)}) collective-permute-start(f32[1,1024]{1,0:T(1,128)S(1)} %get-tuple-element.50), channel_id=1, source_target_pairs={{1,2},{3,4},{5,6},{7,8},{9,10},{11,12},{13,14},{15,16},{17,18},{19... | collective-permute-start | bytes 12296 | tf_op jit(solution)/shard_map/ppermute | solution.py:29
where the time goes:
time: 68.5 us; the launch traced here: 68.6 us
  starting transfers between devices  32.2 us (47%)
  Pallas kernels  19.6 us (29%)
  waiting for transfers between devices  16 us (23%)
  between operations  0.77 us (1%)
    ppermute x8, starting transfers between devices, exchanged(): lax.ppermute(value, AXES, pairs + [(high, low) for low, high in pairs])  32.2 us
    ppermute x8, waiting for transfers between devices, exchanged(): lax.ppermute(value, AXES, pairs + [(high, low) for low, high in pairs])  16 us
    pallas_call x1, Pallas kernels, local_pairs(): pl.pallas_call(local_kernel, out_shape=(shaped((HELD, ROWS, DIM), jnp.bfl...  12 us
    pallas_call x1, Pallas kernels, first_pieces(): pl.pallas_call(first_kernel, out_shape=(piece, piece, shaped((HELD, ROWS)...  2.36 us
    pallas_call x2, Pallas kernels, next_guests(): pl.pallas_call(functools.partial(next_guests_kernel, index), out_shape=(g...  2.04 us
    pallas_call x1, Pallas kernels, first_guests(): pl.pallas_call(first_guests_kernel, out_shape=(guest, guest, shaped((HELD...  1.51 us
  transfers between devices with their start and end apart: 8, of which 4 were waited for; matrix products, arithmetic and copies ran while one was open for 0% of the time, Pallas kernels for 23%

commit v1 on v0

--- a/solution.py
+++ b/solution.py
@@ -13,7 +13,7 @@
 COLS = 256
 LANES = 128
 NOTE = 16
-CUTS = (0, 512, 896, 1024)
+CUTS = ((0, 640, 1024), (0, 640, 1024))
 DIGIT = 128
 DEAD = DIGIT**3 - 1
 NONE = -1e30
@@ -23,14 +23,18 @@
 HBM = pl.BlockSpec(memory_space=pltpu.HBM)
 
 
-def exchanged(value, first):
+def exchanged(value, boundary):
     count = lax.axis_size(AXES)
-    pairs = [(low, low + 1) for low in range(first, count - 1, 2)]
+    pairs = [(low, low + 1) for low in range(boundary, count - 1, 2)]
     return lax.ppermute(value, AXES, pairs + [(high, low) for low, high in pairs])
 
 
 def odd_device():
     return lax.axis_index(AXES[-1]) % 2
+
+
+def cut_rows(boundary, index):
+    return CUTS[boundary][index + 1] - CUTS[boundary][index]
 
 
 def shaped(shape, dtype):
@@ -102,13 +106,13 @@
     return digits[0:1] + digits[1:2] * DIGIT + digits[2:3] * DIGIT**2
 
 
-def piece_copies(index, odd, raw, to_even, to_odd, sems):
-    first, rows = CUTS[index], CUTS[index + 1] - CUTS[index]
-    last_block = HELD - 1
-    return [
-        pltpu.make_async_copy(raw.at[block, pl.ds(first, rows)], piece.at[pl.ds(0, rows)], sems.at[index, side])
-        for side, (block, piece) in enumerate(((last_block * (1 - odd), to_even), (last_block * odd, to_odd)))
-    ]
+def piece_copies(items, raw, pieces, sems):
+    odd, copies = odd_device(), []
+    for number, ((boundary, index), piece) in enumerate(zip(items, pieces)):
+        first, rows = CUTS[boundary][index], cut_rows(boundary, index)
+        block = (HELD - 1) * (odd if boundary else 1 - odd)
+        copies.append(pltpu.make_async_copy(raw.at[block, pl.ds(first, rows)], piece.at[pl.ds(0, rows)], sems.at[number]))
+    return copies
 
 
 def first_kernel(
@@ -116,7 +120,7 @@
     pairs, live, ranks, sems, small_sems,
 ):
     odd = odd_device()
-    copies = piece_copies(0, odd, raw, even_on, odd_on, sems)
+    copies = piece_copies(((0, 0), (1, 0)), raw, (even_on, odd_on), sems)
     small = [
         pltpu.make_async_copy(source, target, small_sems.at[index])
         for index, (source, target) in enumerate(((pairs_hbm, pairs), (live_hbm, live), (ranks_hbm, ranks)))
@@ -140,8 +144,8 @@
     flags[1] = ahead
     note_last = note_rows(keys[HELD - 1 : HELD, :], [])
     note_first = note_rows(keys[0:1, :], [(1 - ahead) * near, far])
-    even_on[pl.ds(CUTS[1], NOTE), :] = jnp.where(odd == 1, note_first, note_last)
-    odd_on[pl.ds(CUTS[1], NOTE), :] = jnp.where(odd == 1, note_last, note_first)
+    even_on[pl.ds(cut_rows(0, 0), NOTE), :] = jnp.where(odd == 1, note_first, note_last)
+    odd_on[pl.ds(cut_rows(1, 0), NOTE), :] = jnp.where(odd == 1, note_last, note_first)
     for copy in copies:
         copy.wait()
 
@@ -151,26 +155,26 @@
 
 
 def first_pieces(pairs, live, ranks, raw):
-    piece = shaped((CUTS[1] + NOTE, DIM), jnp.bfloat16)
+    even, odd = (shaped((cut_rows(boundary, 0) + NOTE, DIM), jnp.bfloat16) for boundary in range(2))
     return pl.pallas_call(
         first_kernel,
-        out_shape=(piece, piece, shaped((HELD, ROWS), jnp.int32), shaped((2,), jnp.int32)),
+        out_shape=(even, odd, shaped((HELD, ROWS), jnp.int32), shaped((2,), jnp.int32)),
         in_specs=[HBM] * 4,
         out_specs=(VMEM,) * 3 + (SMEM,),
         scratch_shapes=[
             pltpu.SMEM(pairs.shape, jnp.int32),
             pltpu.SMEM(live.shape, jnp.int32),
             pltpu.VMEM(ranks.shape, jnp.int32),
-            pltpu.SemaphoreType.DMA((2, 2)),
+            pltpu.SemaphoreType.DMA((2,)),
             pltpu.SemaphoreType.DMA((3,)),
         ],
         compiler_params=pltpu.CompilerParams(vmem_limit_bytes=6 << 20),
-        cost_estimate=pl.CostEstimate(flops=0, bytes_accessed=8 * CUTS[1] * DIM, transcendentals=0),
+        cost_estimate=pl.CostEstimate(flops=0, bytes_accessed=4 * ROWS * DIM, transcendentals=0),
     )(*in_hbm(pairs, live, ranks, raw))
 
 
 def local_kernel(pairs, count, raw, keys, units, best, even_on, odd_on, spread_keys, left_acc, right_acc, sems):
-    copies = piece_copies(1, odd_device(), raw, even_on, odd_on, sems)
+    copies = piece_copies(((0, 1), (1, 1)), raw, (even_on, odd_on), sems)
     for copy in copies:
         copy.start()
     for block in range(HELD):
@@ -216,42 +220,21 @@
 
 
 def local_pairs(pairs, count, raw, keys):
-    piece = shaped((CUTS[2] - CUTS[1], DIM), jnp.bfloat16)
+    even, odd = (shaped((cut_rows(boundary, 1), DIM), jnp.bfloat16) for boundary in range(2))
     return pl.pallas_call(
         local_kernel,
-        out_shape=(shaped((HELD, ROWS, DIM), jnp.bfloat16), shaped((HELD, ROWS), jnp.float32), piece, piece),
+        out_shape=(shaped((HELD, ROWS, DIM), jnp.bfloat16), shaped((HELD, ROWS), jnp.float32), even, odd),
         in_specs=[SMEM, SMEM, VMEM, VMEM],
         out_specs=(VMEM,) * 4,
         scratch_shapes=[
             pltpu.VMEM((HELD, ROWS, LANES), jnp.int32),
             pltpu.VMEM((HELD, ROWS, LANES), jnp.float32),
             pltpu.VMEM((HELD, 8, ROWS), jnp.float32),
-            pltpu.SemaphoreType.DMA((3, 2)),
+            pltpu.SemaphoreType.DMA((2,)),
         ],
         compiler_params=pltpu.CompilerParams(vmem_limit_bytes=24 << 20),
-        cost_estimate=pl.CostEstimate(flops=6 * 2 * ROWS * ROWS * DIM, bytes_accessed=4 * HELD * ROWS * DIM, transcendentals=0),
+        cost_estimate=pl.CostEstimate(flops=2 * ROWS * ROWS * DIM, bytes_accessed=4 * HELD * ROWS * DIM, transcendentals=0),
     )(pairs, count, raw, keys)
-
-
-def last_kernel(raw, after, even_on, odd_on, sems):
-    copies = piece_copies(2, odd_device(), raw, even_on, odd_on, sems)
-    for copy in copies:
-        copy.start()
-    for copy in copies:
-        copy.wait()
-
-
-def last_pieces(raw, after):
-    piece = shaped((CUTS[3] - CUTS[2], DIM), jnp.bfloat16)
-    return pl.pallas_call(
-        last_kernel,
-        out_shape=(piece, piece),
-        in_specs=[HBM, pl.BlockSpec(memory_space=pl.ANY)],
-        out_specs=(VMEM, VMEM),
-        scratch_shapes=[pltpu.SemaphoreType.DMA((3, 2))],
-        compiler_params=pltpu.CompilerParams(vmem_limit_bytes=2 << 20),
-        cost_estimate=pl.CostEstimate(flops=0, bytes_accessed=8 * (CUTS[3] - CUTS[2]) * DIM, transcendentals=0),
-    )(*in_hbm(raw), after)
 
 
 def guest_pairs(flags, after, raw, rows, guest_keys, keys, units, right_acc, guest_units, spread_keys, left_acc):
@@ -305,76 +288,66 @@
     ]
 
 
-def guest_cost(rows, blocks):
-    return pl.CostEstimate(flops=2 * blocks * rows * ROWS * DIM, bytes_accessed=2 * (rows + HELD * ROWS) * DIM, transcendentals=0)
+def guest_cost(rows):
+    return pl.CostEstimate(flops=2 * rows * ROWS * DIM, bytes_accessed=2 * (rows + HELD * ROWS) * DIM, transcendentals=0)
 
 
 def first_guests_kernel(
-    flags, even_raw, odd_raw, keys, units, best_before,
-    even_guest, odd_guest, best, even_keys, odd_keys, even_flags, odd_flags, right_acc, *scratch,
+    boundary, flags, raw, keys, units, best_before, guest_best, best, guest_keys, guest_flags, right_acc, *scratch
 ):
-    odd = odd_device()
-    rows = CUTS[1]
+    rows = cut_rows(boundary, 0)
+    after = odd_device() if boundary else 1 - odd_device()
     right_acc[...] = jnp.full_like(right_acc, NONE)
-    sides = (
-        (1 - odd, even_raw, even_keys, even_flags, even_guest),
-        (odd, odd_raw, odd_keys, odd_flags, odd_guest),
-    )
-    for after, guest_raw, guest_keys, guest_flags, guest_best in sides:
-        note = guest_raw[pl.ds(rows, NOTE), :]
-        guest_keys[...] = noted_keys(note)
-        for which in range(2):
-            noted = (jnp.max(note[3 + which : 4 + which, :].astype(jnp.float32)) > 0.5).astype(jnp.int32)
-            guest_flags[which] = jnp.where(after == 1, noted, flags[which])
-        guest_pairs(guest_flags, after, guest_raw, rows, guest_keys[:, :rows], keys, units, right_acc, *scratch)
-        finish_guests(scratch[-1], 0, None, guest_best)
+    note = raw[pl.ds(rows, NOTE), :]
+    guest_keys[...] = noted_keys(note)
+    for which in range(2):
+        noted = (jnp.max(note[3 + which : 4 + which, :].astype(jnp.float32)) > 0.5).astype(jnp.int32)
+        guest_flags[which] = jnp.where(after == 1, noted, flags[which])
+    guest_pairs(guest_flags, after, raw, rows, guest_keys[:, :rows], keys, units, right_acc, *scratch)
+    finish_guests(scratch[-1], 0, None, guest_best)
     finish_held(right_acc, best_before, best)
 
 
-def first_guests(flags, even_raw, odd_raw, keys, units, best_before):
-    row = shaped((1, ROWS), jnp.int32)
-    two = shaped((2,), jnp.int32)
-    guest = shaped((1, CUTS[1]), jnp.float32)
-    return pl.pallas_call(
-        first_guests_kernel,
-        out_shape=(guest, guest, shaped((HELD, ROWS), jnp.float32), row, row, two, two),
-        in_specs=[SMEM] + [VMEM] * 5,
-        out_specs=(VMEM,) * 5 + (SMEM,) * 2,
-        scratch_shapes=guest_scratch(CUTS[1]),
-        compiler_params=pltpu.CompilerParams(vmem_limit_bytes=16 << 20),
-        cost_estimate=guest_cost(CUTS[1], 3),
-    )(flags, even_raw, odd_raw, keys, units, best_before)
-
-
-def next_guests_kernel(
-    index, even_flags, odd_flags, even_raw, odd_raw, even_keys, odd_keys, keys, units, even_earlier, odd_earlier, best_before,
-    even_guest, odd_guest, best, right_acc, *scratch,
-):
-    first, last = CUTS[index], CUTS[index + 1]
-    odd = odd_device()
-    right_acc[...] = jnp.full_like(right_acc, NONE)
-    sides = (
-        (1 - odd, even_raw, even_keys, even_flags, even_earlier, even_guest),
-        (odd, odd_raw, odd_keys, odd_flags, odd_earlier, odd_guest),
-    )
-    for after, guest_raw, guest_keys, guest_flags, guest_earlier, guest_best in sides:
-        guest_pairs(guest_flags, after, guest_raw, last - first, guest_keys[:, first:last], keys, units, right_acc, *scratch)
-        finish_guests(scratch[-1], first, guest_earlier, guest_best)
-    finish_held(right_acc, best_before, best)
-
-
-def next_guests(index, even_flags, odd_flags, even_raw, odd_raw, even_keys, odd_keys, keys, units, *earlier):
-    guest = shaped((1, CUTS[index + 1]), jnp.float32)
-    rows = CUTS[index + 1] - CUTS[index]
-    return pl.pallas_call(
-        functools.partial(next_guests_kernel, index),
-        out_shape=(guest, guest, shaped((HELD, ROWS), jnp.float32)),
-        in_specs=[SMEM, SMEM] + [VMEM] * 9,
-        out_specs=(VMEM,) * 3,
+def first_guests(boundary, flags, raw, keys, units, best_before):
+    rows = cut_rows(boundary, 0)
+    return pl.pallas_call(
+        functools.partial(first_guests_kernel, boundary),
+        out_shape=(
+            shaped((1, rows), jnp.float32),
+            shaped((HELD, ROWS), jnp.float32),
+            shaped((1, ROWS), jnp.int32),
+            shaped((2,), jnp.int32),
+        ),
+        in_specs=[SMEM] + [VMEM] * 4,
+        out_specs=(VMEM, VMEM, VMEM, SMEM),
         scratch_shapes=guest_scratch(rows),
         compiler_params=pltpu.CompilerParams(vmem_limit_bytes=16 << 20),
-        cost_estimate=guest_cost(rows, 3),
-    )(even_flags, odd_flags, even_raw, odd_raw, even_keys, odd_keys, keys, units, *earlier)
+        cost_estimate=guest_cost(rows),
+    )(flags, raw, keys, units, best_before)
+
+
+def next_guests_kernel(
+    boundary, index, flags, raw, guest_keys, guest_earlier, keys, units, best_before, guest_best, best, right_acc, *scratch
+):
+    first, rows = CUTS[boundary][index], cut_rows(boundary, index)
+    after = odd_device() if boundary else 1 - odd_device()
+    right_acc[...] = jnp.full_like(right_acc, NONE)
+    guest_pairs(flags, after, raw, rows, guest_keys[:, first : first + rows], keys, units, right_acc, *scratch)
+    finish_guests(scratch[-1], first, guest_earlier, guest_best)
+    finish_held(right_acc, best_before, best)
+
+
+def next_guests(boundary, index, flags, *rest):
+    rows = cut_rows(boundary, index)
+    return pl.pallas_call(
+        functools.partial(next_guests_kernel, boundary, index),
+        out_shape=(shaped((1, CUTS[boundary][index + 1]), jnp.float32), shaped((HELD, ROWS), jnp.float32)),
+        in_specs=[SMEM] + [VMEM] * len(rest),
+        out_specs=(VMEM, VMEM),
+        scratch_shapes=guest_scratch(rows),
+        compiler_params=pltpu.CompilerParams(vmem_limit_bytes=16 << 20),
+        cost_estimate=guest_cost(rows),
+    )(flags, *rest)
 
 
 def combined_kernel(keys, best_before, even_found, odd_found, best):
@@ -402,16 +375,13 @@
     even_on, odd_on, keys, flags = first_pieces(pairs, block_rows, ranks, embeddings)
     even_first, odd_first = exchanged(even_on, 0), exchanged(odd_on, 1)
     units, best, even_on, odd_on = local_pairs(pairs, pair_count, embeddings, keys)
-    even_next, odd_next = exchanged(even_on, 0), exchanged(odd_on, 1)
-    even_on, odd_on = last_pieces(embeddings, best)
     even_last, odd_last = exchanged(even_on, 0), exchanged(odd_on, 1)
-    even_guest, odd_guest, best, even_keys, odd_keys, even_flags, odd_flags = first_guests(
-        flags, even_first, odd_first, keys, units, best
-    )
-    known = (even_keys, odd_keys, keys, units)
-    guests = next_guests(1, even_flags, odd_flags, even_next, odd_next, *known, even_guest, odd_guest, best)
-    even_guest, odd_guest, best = next_guests(2, even_flags, odd_flags, even_last, odd_last, *known, *guests)
-    even_found, odd_found = exchanged(even_guest, 0), exchanged(odd_guest, 1)
+    even_guest, best, even_keys, even_flags = first_guests(0, flags, even_first, keys, units, best)
+    odd_guest, best, odd_keys, odd_flags = first_guests(1, flags, odd_first, keys, units, best)
+    even_guest, best = next_guests(0, 1, even_flags, even_last, even_keys, even_guest, keys, units, best)
+    even_found = exchanged(even_guest, 0)
+    odd_guest, best = next_guests(1, 1, odd_flags, odd_last, odd_keys, odd_guest, keys, units, best)
+    odd_found = exchanged(odd_guest, 1)
     return combined(keys, best, even_found, odd_found)
 
 

time: 68.5 us -> 67.2 us (0.981)
  the two profiles are of different devices: /device:TPU:161 before, /device:TPU:131 now
where the time goes in v1:
time: 67.2 us; the launch traced here: 67 us
  waiting for transfers between devices  25.7 us (38%)
  Pallas kernels  23.8 us (35%)
  starting transfers between devices  16.7 us (25%)
  between operations  0.74 us (1%)
    ppermute x6, waiting for transfers between devices, exchanged(): lax.ppermute(value, AXES, pairs + [(high, low) for low, high in pairs])  25.7 us
    ppermute x6, starting transfers between devices, exchanged(): lax.ppermute(value, AXES, pairs + [(high, low) for low, high in pairs])  16.7 us
    pallas_call x1, Pallas kernels, local_pairs(): pl.pallas_call(local_kernel, out_shape=(shaped((HELD, ROWS, DIM), jnp.bfl...  12 us
    pallas_call x2, Pallas kernels, first_guests(): pl.pallas_call(functools.partial(first_guests_kernel, boundary), out_shap...  6.93 us
    pallas_call x1, Pallas kernels, first_pieces(): pl.pallas_call(first_kernel, out_shape=(even, odd, shaped((HELD, ROWS), j...  2.51 us
    pallas_call x2, Pallas kernels, next_guests(): pl.pallas_call(functools.partial(next_guests_kernel, boundary, index), ou...  1.79 us
  transfers between devices with their start and end apart: 6, of which 6 were waited for; matrix products, arithmetic and copies ran while one was open for 0% of the time, Pallas kernels for 30%

profile of v1, /device:TPU:131, one launch (start us, length us, event | category | flops | bytes accessed | tf_op | source)
XLA Modules:
  0.0 67.0 jit_solution(4076265732615285132)
XLA Ops:
  0.0 0.0 copy-start
  0.0 0.0 copy-start.1
  0.0 2.5 %shard_map.55 = (bf16[656,1024]{1,0:T(8,128)(2,1)S(1)}, bf16[656,1024]{1,0:T(8,128)(2,1)S(1)}, s32[3,1024]{1,0:T(4,128)S(1)}, s32[2]{0:T(128)S(1)}) custom-call(s32[1,2,6]{2,1,0:T(2,128)} %bitcast.1, s32[3]{0:T(128)} %live_hbm.1, s32[3,1024]{1,0:T(4,128)} %ranks_hbm.1, bf16[3,1024,1024]{2,1,0:T(8,128)(2,1)} %raw.3), custom_call_target="tpu_custom_call" | custom-call | bytes 4194304 | tf_op jit(solution)/shard_map/pallas_call | solution.py:159
  2.5 1.4 %collective-permute-start.1 = (bf16[656,1024]{1,0:T(8,128)(2,1)S(1)}, bf16[656,1024]{1,0:T(8,128)(2,1)S(1)}, u32[]{:S(2)}, u32[]{:S(2)}) collective-permute-start(bf16[656,1024]{1,0:T(8,128)(2,1)S(1)} %get-tuple-element.29), channel_id=1, source_target_pairs={{0,1},{2,3},{4,5},{6,7},{8,9},{10,11},{12,13},{14,15},{16,17},{18,... | collective-permute-start | bytes 4030472 | tf_op jit(solution)/shard_map/ppermute | solution.py:29
  3.9 4.6 %collective-permute-start = (bf16[656,1024]{1,0:T(8,128)(2,1)S(1)}, bf16[656,1024]{1,0:T(8,128)(2,1)S(1)}, u32[]{:S(2)}, u32[]{:S(2)}) collective-permute-start(bf16[656,1024]{1,0:T(8,128)(2,1)S(1)} %get-tuple-element.27), channel_id=1, source_target_pairs={{1,2},{3,4},{5,6},{7,8},{9,10},{11,12},{13,14},{15,16},{17,18},{19... | collective-permute-start | bytes 4030472 | tf_op jit(solution)/shard_map/ppermute | solution.py:29
  9.2 0.0 copy-done
  9.2 0.0 copy-done.1
  9.2 12.0 %shard_map.56 = (bf16[3,1024,1024]{2,1,0:T(8,128)(2,1)S(1)}, f32[3,1024]{1,0:T(4,128)S(1)}, bf16[384,1024]{1,0:T(8,128)(2,1)S(1)}, bf16[384,1024]{1,0:T(8,128)(2,1)S(1)}) custom-call(s32[1,2,6]{2,1,0:T(2,128)S(1)} %bitcast.2, s32[1]{0:T(128)S(6)} %copy.6.count, bf16[3,1024,1024]{2,1,0:T(8,128)(2,1)S(1)} %copy-done, s32[3,1024]{1,0:T(4,128)S(1)} %get-tuple-element.25.keys), custom_call_target="tpu_custom_call" | custom-call | flops 2147483648 | bytes 12582912 | tf_op jit(solution)/shard_map/pallas_call | solution.py:224
  21.2 0.1 collective-permute-start.3
  21.3 3.2 %collective-permute-start.2 = (bf16[384,1024]{1,0:T(8,128)(2,1)S(1)}, bf16[384,1024]{1,0:T(8,128)(2,1)S(1)}, u32[]{:S(2)}, u32[]{:S(2)}) collective-permute-start(bf16[384,1024]{1,0:T(8,128)(2,1)S(1)} %get-tuple-element.33), channel_id=1, source_target_pairs={{1,2},{3,4},{5,6},{7,8},{9,10},{11,12},{13,14},{15,16},{17,18},{19... | collective-permute-start | bytes 2359304 | tf_op jit(solution)/shard_map/ppermute | solution.py:29
  24.5 8.5 %collective-permute-done.1.raw = bf16[656,1024]{1,0:T(8,128)(2,1)S(1)} collective-permute-done((bf16[656,1024]{1,0:T(8,128)(2,1)S(1)}, bf16[656,1024]{1,0:T(8,128)(2,1)S(1)}, u32[]{:S(2)}, u32[]{:S(2)}) %collective-permute-start.1) | collective-permute-done | bytes 1343520 | tf_op jit(solution)/shard_map/ppermute | solution.py:29
  33.0 5.6 %shard_map.57 = (f32[1,640]{1,0:T(1,128)S(1)}, f32[3,1024]{1,0:T(4,128)S(1)}, s32[1,1024]{1,0:T(1,128)S(1)}, s32[2]{0:T(128)S(1)}) custom-call(s32[2]{0:T(128)S(1)} %get-tuple-element.26.flags, bf16[656,1024]{1,0:T(8,128)(2,1)S(1)} %collective-permute-done.1.raw, s32[3,1024]{1,0:T(4,128)S(1)} %get-tuple-element.25.keys, ...), custom_call_target="tpu_custom_call" | custom-call | flops 1342177280 | bytes 7602176 | tf_op jit(solution)/shard_map/pallas_call | solution.py:313
  38.6 8.6 %collective-permute-done.raw = bf16[656,1024]{1,0:T(8,128)(2,1)S(1)} collective-permute-done((bf16[656,1024]{1,0:T(8,128)(2,1)S(1)}, bf16[656,1024]{1,0:T(8,128)(2,1)S(1)}, u32[]{:S(2)}, u32[]{:S(2)}) %collective-permute-start) | collective-permute-done | bytes 1343520 | tf_op jit(solution)/shard_map/ppermute | solution.py:29
  47.2 1.3 %shard_map.58 = (f32[1,640]{1,0:T(1,128)S(1)}, f32[3,1024]{1,0:T(4,128)S(1)}, s32[1,1024]{1,0:T(1,128)S(1)}, s32[2]{0:T(128)S(1)}) custom-call(s32[2]{0:T(128)S(1)} %get-tuple-element.26.flags, bf16[656,1024]{1,0:T(8,128)(2,1)S(1)} %collective-permute-done.raw, s32[3,1024]{1,0:T(4,128)S(1)} %get-tuple-element.25.keys, ...), custom_call_target="tpu_custom_call" | custom-call | flops 1342177280 | bytes 7602176 | tf_op jit(solution)/shard_map/pallas_call | solution.py:313
  48.5 1.3 %collective-permute-done.3.raw = bf16[384,1024]{1,0:T(8,128)(2,1)S(1)} collective-permute-done((bf16[384,1024]{1,0:T(8,128)(2,1)S(1)}, bf16[384,1024]{1,0:T(8,128)(2,1)S(1)}, u32[]{:S(2)}, u32[]{:S(2)}) %collective-permute-start.3) | collective-permute-done | bytes 786464 | tf_op jit(solution)/shard_map/ppermute | solution.py:29
  49.8 1.0 %shard_map.59 = (f32[1,1024]{1,0:T(1,128)S(1)}, f32[3,1024]{1,0:T(4,128)S(1)}) custom-call(s32[2]{0:T(128)S(1)} %get-tuple-element.36.flags, bf16[384,1024]{1,0:T(8,128)(2,1)S(1)} %collective-permute-done.3.raw, s32[1,1024]{1,0:T(1,128)S(1)} %get-tuple-element.38.guest_keys, f32[1,640]{1,0:T(1,128)S(1)} %get-tuple-element.39.guest_earlier, ...), custom_call_target="tpu_custom_call" | custom-call | flops 805306368 | bytes 7077888 | tf_op jit(solution)/shard_map/pallas_call | solution.py:342
  50.8 4.8 %collective-permute-done.2.raw = bf16[384,1024]{1,0:T(8,128)(2,1)S(1)} collective-permute-done((bf16[384,1024]{1,0:T(8,128)(2,1)S(1)}, bf16[384,1024]{1,0:T(8,128)(2,1)S(1)}, u32[]{:S(2)}, u32[]{:S(2)}) %collective-permute-start.2) | collective-permute-done | bytes 786464 | tf_op jit(solution)/shard_map/ppermute | solution.py:29
  55.6 0.8 %shard_map.60 = (f32[1,1024]{1,0:T(1,128)S(1)}, f32[3,1024]{1,0:T(4,128)S(1)}) custom-call(s32[2]{0:T(128)S(1)} %get-tuple-element.32.flags, bf16[384,1024]{1,0:T(8,128)(2,1)S(1)} %collective-permute-done.2.raw, s32[1,1024]{1,0:T(1,128)S(1)} %get-tuple-element.34.guest_keys, f32[1,640]{1,0:T(1,128)S(1)} %get-tuple-element.35.guest_earlier, ...), custom_call_target="tpu_custom_call" | custom-call | flops 805306368 | bytes 7077888 | tf_op jit(solution)/shard_map/pallas_call | solution.py:342
  56.4 7.4 %collective-permute-start.5 = (f32[1,1024]{1,0:T(1,128)S(1)}, f32[1,1024]{1,0:T(1,128)S(1)}, u32[]{:S(2)}, u32[]{:S(2)}) collective-permute-start(f32[1,1024]{1,0:T(1,128)S(1)} %get-tuple-element.44), channel_id=1, source_target_pairs={{1,2},{3,4},{5,6},{7,8},{9,10},{11,12},{13,14},{15,16},{17,18},{19... | collective-permute-start | bytes 12296 | tf_op jit(solution)/shard_map/ppermute | solution.py:29
  63.8 0.1 collective-permute-start.4
  63.9 1.2 %collective-permute-done.5.odd_found = f32[1,1024]{1,0:T(1,128)S(1)} collective-permute-done((f32[1,1024]{1,0:T(1,128)S(1)}, f32[1,1024]{1,0:T(1,128)S(1)}, u32[]{:S(2)}, u32[]{:S(2)}) %collective-permute-start.5) | collective-permute-done | bytes 4128 | tf_op jit(solution)/shard_map/ppermute | solution.py:29
  65.1 1.3 %collective-permute-done.4.even_found = f32[1,1024]{1,0:T(1,128)S(1)} collective-permute-done((f32[1,1024]{1,0:T(1,128)S(1)}, f32[1,1024]{1,0:T(1,128)S(1)}, u32[]{:S(2)}, u32[]{:S(2)}) %collective-permute-start.4) | collective-permute-done | bytes 4128 | tf_op jit(solution)/shard_map/ppermute | solution.py:29
  66.4 0.6 shard_map.61
Async XLA Ops:
  0.0 9.2 %copy-start = (bf16[3,1024,1024]{2,1,0:T(8,128)(2,1)S(1)}, bf16[3,1024,1024]{2,1,0:T(8,128)(2,1)}, u32[]{:S(2)}) copy-start(bf16[3,1024,1024]{2,1,0:T(8,128)(2,1)} %raw.3) | copy-start | bytes 18874372
  0.0 9.2 %copy-start.1 = (s32[1,6,2]{1,2,0:T(2,128)S(1)}, s32[1,6,2]{1,2,0:T(2,128)}, u32[]{:S(2)}) copy-start(s32[1,6,2]{1,2,0:T(2,128)} %param.8) | copy-start | bytes 148
  2.5 30.4 %collective-permute-start.1 = (bf16[656,1024]{1,0:T(8,128)(2,1)S(1)}, bf16[656,1024]{1,0:T(8,128)(2,1)S(1)}, u32[]{:S(2)}, u32[]{:S(2)}) collective-permute-start(bf16[656,1024]{1,0:T(8,128)(2,1)S(1)} %get-tuple-element.29), channel_id=1, source_target_pairs={{0,1},{2,3},{4,5},{6,7},{8,9},{10,11},{12,13},{14,15},{16,17},{18,... | collective-permute-start | bytes 4030472 | tf_op jit(solution)/shard_map/ppermute | solution.py:29
  3.9 43.3 %collective-permute-start = (bf16[656,1024]{1,0:T(8,128)(2,1)S(1)}, bf16[656,1024]{1,0:T(8,128)(2,1)S(1)}, u32[]{:S(2)}, u32[]{:S(2)}) collective-permute-start(bf16[656,1024]{1,0:T(8,128)(2,1)S(1)} %get-tuple-element.27), channel_id=1, source_target_pairs={{1,2},{3,4},{5,6},{7,8},{9,10},{11,12},{13,14},{15,16},{17,18},{19... | collective-permute-start | bytes 4030472 | tf_op jit(solution)/shard_map/ppermute | solution.py:29
  21.2 28.6 %collective-permute-start.3 = (bf16[384,1024]{1,0:T(8,128)(2,1)S(1)}, bf16[384,1024]{1,0:T(8,128)(2,1)S(1)}, u32[]{:S(2)}, u32[]{:S(2)}) collective-permute-start(bf16[384,1024]{1,0:T(8,128)(2,1)S(1)} %get-tuple-element.37), channel_id=1, source_target_pairs={{0,1},{2,3},{4,5},{6,7},{8,9},{10,11},{12,13},{14,15},{16,17},{18,... | collective-permute-start | bytes 2359304 | tf_op jit(solution)/shard_map/ppermute | solution.py:29
  21.3 34.3 %collective-permute-start.2 = (bf16[384,1024]{1,0:T(8,128)(2,1)S(1)}, bf16[384,1024]{1,0:T(8,128)(2,1)S(1)}, u32[]{:S(2)}, u32[]{:S(2)}) collective-permute-start(bf16[384,1024]{1,0:T(8,128)(2,1)S(1)} %get-tuple-element.33), channel_id=1, source_target_pairs={{1,2},{3,4},{5,6},{7,8},{9,10},{11,12},{13,14},{15,16},{17,18},{19... | collective-permute-start | bytes 2359304 | tf_op jit(solution)/shard_map/ppermute | solution.py:29
  56.4 8.7 %collective-permute-start.5 = (f32[1,1024]{1,0:T(1,128)S(1)}, f32[1,1024]{1,0:T(1,128)S(1)}, u32[]{:S(2)}, u32[]{:S(2)}) collective-permute-start(f32[1,1024]{1,0:T(1,128)S(1)} %get-tuple-element.44), channel_id=1, source_target_pairs={{1,2},{3,4},{5,6},{7,8},{9,10},{11,12},{13,14},{15,16},{17,18},{19... | collective-permute-start | bytes 12296 | tf_op jit(solution)/shard_map/ppermute | solution.py:29
  63.8 2.5 %collective-permute-start.4 = (f32[1,1024]{1,0:T(1,128)S(1)}, f32[1,1024]{1,0:T(1,128)S(1)}, u32[]{:S(2)}, u32[]{:S(2)}) collective-permute-start(f32[1,1024]{1,0:T(1,128)S(1)} %get-tuple-element.43), channel_id=1, source_target_pairs={{0,1},{2,3},{4,5},{6,7},{8,9},{10,11},{12,13},{14,15},{16,17},{18,... | collective-permute-start | bytes 12296 | tf_op jit(solution)/shard_map/ppermute | solution.py:29

commit v2 on v1

--- a/solution.py
+++ b/solution.py
@@ -31,6 +31,10 @@
 
 def odd_device():
     return lax.axis_index(AXES[-1]) % 2
+
+
+def odd_after(boundary):
+    return odd_device() if boundary else 1 - odd_device()
 
 
 def cut_rows(boundary, index):
@@ -115,9 +119,20 @@
     return copies
 
 
+def boundary_flags(pairs):
+    def listed(u, v):
+        found = jnp.int32(0)
+        for slot in range(pairs.shape[2]):
+            found = found | ((pairs[0, 0, slot] == u) & (pairs[0, 1, slot] == v)).astype(jnp.int32)
+        return found
+
+    ahead, near, far = listed(HELD + 1, HELD - 1), listed(HELD, HELD - 1), listed(HELD, HELD - 2)
+    here, there = ahead * near, (1 - ahead) * near
+    return [here, ahead, there], [there, far, here]
+
+
 def first_kernel(
-    pairs_hbm, live_hbm, ranks_hbm, raw, even_on, odd_on, keys, flags,
-    pairs, live, ranks, sems, small_sems,
+    pairs_hbm, live_hbm, ranks_hbm, raw, even_on, odd_on, keys, pairs, live, ranks, sems, small_sems
 ):
     odd = odd_device()
     copies = piece_copies(((0, 0), (1, 0)), raw, (even_on, odd_on), sems)
@@ -133,17 +148,9 @@
     for block in range(HELD):
         keys[block : block + 1, :] = jnp.where(position < live[block], ranks[block : block + 1, :], DEAD)
 
-    def listed(u, v):
-        found = jnp.int32(0)
-        for slot in range(pairs.shape[2]):
-            found = found | ((pairs[0, 0, slot] == u) & (pairs[0, 1, slot] == v)).astype(jnp.int32)
-        return found
-
-    ahead, near, far = listed(HELD + 1, HELD - 1), listed(HELD, HELD - 1), listed(HELD, HELD - 2)
-    flags[0] = ahead * near
-    flags[1] = ahead
+    left_flags, right_flags = boundary_flags(pairs)
     note_last = note_rows(keys[HELD - 1 : HELD, :], [])
-    note_first = note_rows(keys[0:1, :], [(1 - ahead) * near, far])
+    note_first = note_rows(keys[0:1, :], right_flags)
     even_on[pl.ds(cut_rows(0, 0), NOTE), :] = jnp.where(odd == 1, note_first, note_last)
     odd_on[pl.ds(cut_rows(1, 0), NOTE), :] = jnp.where(odd == 1, note_last, note_first)
     for copy in copies:
@@ -158,9 +165,9 @@
     even, odd = (shaped((cut_rows(boundary, 0) + NOTE, DIM), jnp.bfloat16) for boundary in range(2))
     return pl.pallas_call(
         first_kernel,
-        out_shape=(even, odd, shaped((HELD, ROWS), jnp.int32), shaped((2,), jnp.int32)),
+        out_shape=(even, odd, shaped((HELD, ROWS), jnp.int32)),
         in_specs=[HBM] * 4,
-        out_specs=(VMEM,) * 3 + (SMEM,),
+        out_specs=(VMEM,) * 3,
         scratch_shapes=[
             pltpu.SMEM(pairs.shape, jnp.int32),
             pltpu.SMEM(live.shape, jnp.int32),
@@ -173,10 +180,12 @@
     )(*in_hbm(pairs, live, ranks, raw))
 
 
-def local_kernel(pairs, count, raw, keys, units, best, even_on, odd_on, spread_keys, left_acc, right_acc, sems):
+def local_kernel(pairs, count, raw, keys, units, best, even_on, odd_on, flags, spread_keys, left_acc, right_acc, sems):
     copies = piece_copies(((0, 1), (1, 1)), raw, (even_on, odd_on), sems)
     for copy in copies:
         copy.start()
+    for index, flag in enumerate(boundary_flags(pairs)[0]):
+        flags[index] = flag
     for block in range(HELD):
         for group in range(ROWS // LANES):
             rows = pl.ds(group * LANES, LANES)
@@ -223,9 +232,15 @@
     even, odd = (shaped((cut_rows(boundary, 1), DIM), jnp.bfloat16) for boundary in range(2))
     return pl.pallas_call(
         local_kernel,
-        out_shape=(shaped((HELD, ROWS, DIM), jnp.bfloat16), shaped((HELD, ROWS), jnp.float32), even, odd),
+        out_shape=(
+            shaped((HELD, ROWS, DIM), jnp.bfloat16),
+            shaped((HELD, ROWS), jnp.float32),
+            even,
+            odd,
+            shaped((3,), jnp.int32),
+        ),
         in_specs=[SMEM, SMEM, VMEM, VMEM],
-        out_specs=(VMEM,) * 4,
+        out_specs=(VMEM,) * 4 + (SMEM,),
         scratch_shapes=[
             pltpu.VMEM((HELD, ROWS, LANES), jnp.int32),
             pltpu.VMEM((HELD, ROWS, LANES), jnp.float32),
@@ -237,12 +252,23 @@
     )(pairs, count, raw, keys)
 
 
-def guest_pairs(flags, after, raw, rows, guest_keys, keys, units, right_acc, guest_units, spread_keys, left_acc):
-    cols = max(COLS, min(ROWS, COLS * ROWS // rows // COLS * COLS))
+def guest_pairs(boundary, index, flags, raw, guest_keys, keys, units, right_acc, guest_units, spread_keys, left_acc):
+    first, rows = CUTS[boundary][index], cut_rows(boundary, index)
+    guest_keys = guest_keys[:, first : first + rows]
+    beside = (HELD - 1) * (odd_after(boundary))
+    cols = max(COLS, COLS * ROWS // rows // COLS * COLS)
     left_acc[...] = jnp.full_like(left_acc, NONE)
     some_live = jnp.min(guest_keys[:, :LANES].astype(jnp.float32)) < DEAD
-
-    @pl.when(((flags[0] != 0) | (flags[1] != 0)) & some_live)
+    takes_beside = flags[0] if index == 0 else jnp.int32(0)
+
+    def meet(block, low, high, width):
+        for col in range(low, high, width):
+            pair_strip(
+                0, guest_units, spread_keys, left_acc,
+                units.at[block], keys.at[pl.ds(block, 1)], right_acc.at[block], pl.ds(col, width),
+            )
+
+    @pl.when(((takes_beside != 0) | (flags[1] != 0) | (flags[2] != 0)) & some_live)
     def _():
         normalize(raw, guest_units, rows)
         for group in range(rows // LANES):
@@ -250,19 +276,18 @@
             spread_keys[at, :] = spread(guest_keys[:, group * LANES : (group + 1) * LANES])
 
         def visit(which, carry):
-            block = which + after * (HELD - 1 - 2 * which)
-
             @pl.when(flags[which] != 0)
             def _():
-                for col in range(0, ROWS, cols):
-                    pair_strip(
-                        0, guest_units, spread_keys, left_acc,
-                        units.at[block], keys.at[pl.ds(block, 1)], right_acc.at[block], pl.ds(col, cols),
-                    )
+                meet(jnp.where(which == 0, beside, 1), 0, ROWS, cols)
 
             return carry
 
-        lax.fori_loop(0, 2, visit, 0)
+        lax.fori_loop(0 if index == 0 else 1, 2, visit, 0)
+
+        @pl.when(flags[2] != 0)
+        def _():
+            low = CUTS[boundary][-2]
+            meet(beside, low, ROWS, ROWS - low)
 
 
 def finish_guests(left_acc, first, guest_earlier, guest_best):
@@ -296,14 +321,14 @@
     boundary, flags, raw, keys, units, best_before, guest_best, best, guest_keys, guest_flags, right_acc, *scratch
 ):
     rows = cut_rows(boundary, 0)
-    after = odd_device() if boundary else 1 - odd_device()
+    after = odd_after(boundary)
     right_acc[...] = jnp.full_like(right_acc, NONE)
     note = raw[pl.ds(rows, NOTE), :]
     guest_keys[...] = noted_keys(note)
-    for which in range(2):
+    for which in range(3):
         noted = (jnp.max(note[3 + which : 4 + which, :].astype(jnp.float32)) > 0.5).astype(jnp.int32)
         guest_flags[which] = jnp.where(after == 1, noted, flags[which])
-    guest_pairs(guest_flags, after, raw, rows, guest_keys[:, :rows], keys, units, right_acc, *scratch)
+    guest_pairs(boundary, 0, guest_flags, raw, guest_keys, keys, units, right_acc, *scratch)
     finish_guests(scratch[-1], 0, None, guest_best)
     finish_held(right_acc, best_before, best)
 
@@ -316,7 +341,7 @@
             shaped((1, rows), jnp.float32),
             shaped((HELD, ROWS), jnp.float32),
             shaped((1, ROWS), jnp.int32),
-            shaped((2,), jnp.int32),
+            shaped((3,), jnp.int32),
         ),
         in_specs=[SMEM] + [VMEM] * 4,
         out_specs=(VMEM, VMEM, VMEM, SMEM),
@@ -329,11 +354,9 @@
 def next_guests_kernel(
     boundary, index, flags, raw, guest_keys, guest_earlier, keys, units, best_before, guest_best, best, right_acc, *scratch
 ):
-    first, rows = CUTS[boundary][index], cut_rows(boundary, index)
-    after = odd_device() if boundary else 1 - odd_device()
     right_acc[...] = jnp.full_like(right_acc, NONE)
-    guest_pairs(flags, after, raw, rows, guest_keys[:, first : first + rows], keys, units, right_acc, *scratch)
-    finish_guests(scratch[-1], first, guest_earlier, guest_best)
+    guest_pairs(boundary, index, flags, raw, guest_keys, keys, units, right_acc, *scratch)
+    finish_guests(scratch[-1], CUTS[boundary][index], guest_earlier, guest_best)
     finish_held(right_acc, best_before, best)
 
 
@@ -372,9 +395,9 @@
 
 def local(embeddings, ranks, block_rows, pair_list, pair_count):
     pairs = pair_list.transpose(0, 2, 1)
-    even_on, odd_on, keys, flags = first_pieces(pairs, block_rows, ranks, embeddings)
+    even_on, odd_on, keys = first_pieces(pairs, block_rows, ranks, embeddings)
     even_first, odd_first = exchanged(even_on, 0), exchanged(odd_on, 1)
-    units, best, even_on, odd_on = local_pairs(pairs, pair_count, embeddings, keys)
+    units, best, even_on, odd_on, flags = local_pairs(pairs, pair_count, embeddings, keys)
     even_last, odd_last = exchanged(even_on, 0), exchanged(odd_on, 1)
     even_guest, best, even_keys, even_flags = first_guests(0, flags, even_first, keys, units, best)
     odd_guest, best, odd_keys, odd_flags = first_guests(1, flags, odd_first, keys, units, best)

time: 67.2 us -> 65.3 us (0.972)
  the two profiles are of different devices: /device:TPU:131 before, /device:TPU:103 now
where the time goes in v2:
time: 65.3 us; the launch traced here: 64.6 us
  Pallas kernels  25.3 us (39%)
  waiting for transfers between devices  21.3 us (33%)
  starting transfers between devices  17.2 us (26%)
  between operations  0.74 us (1%)
    ppermute x6, waiting for transfers between devices, exchanged(): lax.ppermute(value, AXES, pairs + [(high, low) for low, high in pairs])  21.3 us
    ppermute x6, starting transfers between devices, exchanged(): lax.ppermute(value, AXES, pairs + [(high, low) for low, high in pairs])  17.2 us
    pallas_call x1, Pallas kernels, local_pairs(): pl.pallas_call(local_kernel, out_shape=(shaped((HELD, ROWS, DIM), jnp.bfl...  12.5 us
    pallas_call x2, Pallas kernels, first_guests(): pl.pallas_call(functools.partial(first_guests_kernel, boundary), out_shap...  7.11 us
    pallas_call x2, Pallas kernels, next_guests(): pl.pallas_call(functools.partial(next_guests_kernel, boundary, index), ou...  3.12 us
    pallas_call x1, Pallas kernels, first_pieces(): pl.pallas_call(first_kernel, out_shape=(even, odd, shaped((HELD, ROWS), j...  1.92 us
  transfers between devices with their start and end apart: 6, of which 5 were waited for; matrix products, arithmetic and copies ran while one was open for 0% of the time, Pallas kernels for 32%

profile of v2, /device:TPU:103, one launch (start us, length us, event | category | flops | bytes accessed | tf_op | source)
XLA Modules:
  0.0 64.6 jit_solution(12189264804326411301)
XLA Ops:
  0.0 0.0 copy-start
  0.0 0.0 copy-start.1
  0.0 1.9 %shard_map.55 = (bf16[656,1024]{1,0:T(8,128)(2,1)S(1)}, bf16[656,1024]{1,0:T(8,128)(2,1)S(1)}, s32[3,1024]{1,0:T(4,128)S(1)}) custom-call(s32[1,2,6]{2,1,0:T(2,128)} %bitcast.1, s32[3]{0:T(128)} %live_hbm.1, s32[3,1024]{1,0:T(4,128)} %ranks_hbm.1, bf16[3,1024,1024]{2,1,0:T(8,128)(2,1)} %raw.3), custom_call_target="tpu_custom_call" | custom-call | bytes 4194304 | tf_op jit(solution)/shard_map/pallas_call | solution.py:166
  1.9 1.4 %collective-permute-start.1 = (bf16[656,1024]{1,0:T(8,128)(2,1)S(1)}, bf16[656,1024]{1,0:T(8,128)(2,1)S(1)}, u32[]{:S(2)}, u32[]{:S(2)}) collective-permute-start(bf16[656,1024]{1,0:T(8,128)(2,1)S(1)} %get-tuple-element.29), channel_id=1, source_target_pairs={{0,1},{2,3},{4,5},{6,7},{8,9},{10,11},{12,13},{14,15},{16,17},{18,... | collective-permute-start | bytes 4030472 | tf_op jit(solution)/shard_map/ppermute | solution.py:29
  3.3 4.6 %collective-permute-start = (bf16[656,1024]{1,0:T(8,128)(2,1)S(1)}, bf16[656,1024]{1,0:T(8,128)(2,1)S(1)}, u32[]{:S(2)}, u32[]{:S(2)}) collective-permute-start(bf16[656,1024]{1,0:T(8,128)(2,1)S(1)} %get-tuple-element.27), channel_id=1, source_target_pairs={{1,2},{3,4},{5,6},{7,8},{9,10},{11,12},{13,14},{15,16},{17,18},{19... | collective-permute-start | bytes 4030472 | tf_op jit(solution)/shard_map/ppermute | solution.py:29
  8.6 0.0 copy-done
  8.6 0.0 copy-done.1
  8.6 12.5 %shard_map.56 = (bf16[3,1024,1024]{2,1,0:T(8,128)(2,1)S(1)}, f32[3,1024]{1,0:T(4,128)S(1)}, bf16[384,1024]{1,0:T(8,128)(2,1)S(1)}, bf16[384,1024]{1,0:T(8,128)(2,1)S(1)}, s32[3]{0:T(128)S(1)}) custom-call(s32[1,2,6]{2,1,0:T(2,128)S(1)} %bitcast.2, s32[1]{0:T(128)S(6)} %copy.6.count, bf16[3,1024,1024]{2,1,0:T(8,128)(2,1)S(1)} %copy-done, ...), custom_call_target="tpu_custom_call" | custom-call | flops 2147483648 | bytes 12582912 | tf_op jit(solution)/shard_map/pallas_call | solution.py:233
  21.2 5.1 %collective-permute-start.3 = (bf16[384,1024]{1,0:T(8,128)(2,1)S(1)}, bf16[384,1024]{1,0:T(8,128)(2,1)S(1)}, u32[]{:S(2)}, u32[]{:S(2)}) collective-permute-start(bf16[384,1024]{1,0:T(8,128)(2,1)S(1)} %get-tuple-element.37), channel_id=1, source_target_pairs={{0,1},{2,3},{4,5},{6,7},{8,9},{10,11},{12,13},{14,15},{16,17},{18,... | collective-permute-start | bytes 2359304 | tf_op jit(solution)/shard_map/ppermute | solution.py:29
  26.3 1.9 %collective-permute-start.2 = (bf16[384,1024]{1,0:T(8,128)(2,1)S(1)}, bf16[384,1024]{1,0:T(8,128)(2,1)S(1)}, u32[]{:S(2)}, u32[]{:S(2)}) collective-permute-start(bf16[384,1024]{1,0:T(8,128)(2,1)S(1)} %get-tuple-element.33), channel_id=1, source_target_pairs={{1,2},{3,4},{5,6},{7,8},{9,10},{11,12},{13,14},{15,16},{17,18},{19... | collective-permute-start | bytes 2359304 | tf_op jit(solution)/shard_map/ppermute | solution.py:29
  28.2 4.1 %collective-permute-done.1.raw = bf16[656,1024]{1,0:T(8,128)(2,1)S(1)} collective-permute-done((bf16[656,1024]{1,0:T(8,128)(2,1)S(1)}, bf16[656,1024]{1,0:T(8,128)(2,1)S(1)}, u32[]{:S(2)}, u32[]{:S(2)}) %collective-permute-start.1) | collective-permute-done | bytes 1343520 | tf_op jit(solution)/shard_map/ppermute | solution.py:29
  32.4 1.3 %shard_map.57 = (f32[1,640]{1,0:T(1,128)S(1)}, f32[3,1024]{1,0:T(4,128)S(1)}, s32[1,1024]{1,0:T(1,128)S(1)}, s32[3]{0:T(128)S(1)}) custom-call(s32[3]{0:T(128)S(1)} %get-tuple-element.26.flags, bf16[656,1024]{1,0:T(8,128)(2,1)S(1)} %collective-permute-done.1.raw, s32[3,1024]{1,0:T(4,128)S(1)} %get-tuple-element.25.keys, ...), custom_call_target="tpu_custom_call" | custom-call | flops 1342177280 | bytes 7602176 | tf_op jit(solution)/shard_map/pallas_call | solution.py:338
  33.7 13.0 %collective-permute-done.raw = bf16[656,1024]{1,0:T(8,128)(2,1)S(1)} collective-permute-done((bf16[656,1024]{1,0:T(8,128)(2,1)S(1)}, bf16[656,1024]{1,0:T(8,128)(2,1)S(1)}, u32[]{:S(2)}, u32[]{:S(2)}) %collective-permute-start) | collective-permute-done | bytes 1343520 | tf_op jit(solution)/shard_map/ppermute | solution.py:29
  46.6 5.8 %shard_map.58 = (f32[1,640]{1,0:T(1,128)S(1)}, f32[3,1024]{1,0:T(4,128)S(1)}, s32[1,1024]{1,0:T(1,128)S(1)}, s32[3]{0:T(128)S(1)}) custom-call(s32[3]{0:T(128)S(1)} %get-tuple-element.26.flags, bf16[656,1024]{1,0:T(8,128)(2,1)S(1)} %collective-permute-done.raw, s32[3,1024]{1,0:T(4,128)S(1)} %get-tuple-element.25.keys, ...), custom_call_target="tpu_custom_call" | custom-call | flops 1342177280 | bytes 7602176 | tf_op jit(solution)/shard_map/pallas_call | solution.py:338
  52.5 0.0 collective-permute-done.3.raw
  52.5 0.8 %shard_map.59 = (f32[1,1024]{1,0:T(1,128)S(1)}, f32[3,1024]{1,0:T(4,128)S(1)}) custom-call(s32[3]{0:T(128)S(1)} %get-tuple-element.36.flags, bf16[384,1024]{1,0:T(8,128)(2,1)S(1)} %collective-permute-done.3.raw, s32[1,1024]{1,0:T(1,128)S(1)} %get-tuple-element.38.guest_keys, f32[1,640]{1,0:T(1,128)S(1)} %get-tuple-element.39.guest_earlier, ...), custom_call_target="tpu_custom_call" | custom-call | flops 805306368 | bytes 7077888 | tf_op jit(solution)/shard_map/pallas_call | solution.py:365
  53.3 1.8 %collective-permute-done.2.raw = bf16[384,1024]{1,0:T(8,128)(2,1)S(1)} collective-permute-done((bf16[384,1024]{1,0:T(8,128)(2,1)S(1)}, bf16[384,1024]{1,0:T(8,128)(2,1)S(1)}, u32[]{:S(2)}, u32[]{:S(2)}) %collective-permute-start.2) | collective-permute-done | bytes 786464 | tf_op jit(solution)/shard_map/ppermute | solution.py:29
  55.0 2.3 %shard_map.60 = (f32[1,1024]{1,0:T(1,128)S(1)}, f32[3,1024]{1,0:T(4,128)S(1)}) custom-call(s32[3]{0:T(128)S(1)} %get-tuple-element.32.flags, bf16[384,1024]{1,0:T(8,128)(2,1)S(1)} %collective-permute-done.2.raw, s32[1,1024]{1,0:T(1,128)S(1)} %get-tuple-element.34.guest_keys, f32[1,640]{1,0:T(1,128)S(1)} %get-tuple-element.35.guest_earlier, ...), custom_call_target="tpu_custom_call" | custom-call | flops 805306368 | bytes 7077888 | tf_op jit(solution)/shard_map/pallas_call | solution.py:365
  57.4 4.1 %collective-permute-start.5 = (f32[1,1024]{1,0:T(1,128)S(1)}, f32[1,1024]{1,0:T(1,128)S(1)}, u32[]{:S(2)}, u32[]{:S(2)}) collective-permute-start(f32[1,1024]{1,0:T(1,128)S(1)} %get-tuple-element.44), channel_id=1, source_target_pairs={{1,2},{3,4},{5,6},{7,8},{9,10},{11,12},{13,14},{15,16},{17,18},{19... | collective-permute-start | bytes 12296 | tf_op jit(solution)/shard_map/ppermute | solution.py:29
  61.4 0.1 collective-permute-start.4
  61.5 2.0 %collective-permute-done.5.odd_found = f32[1,1024]{1,0:T(1,128)S(1)} collective-permute-done((f32[1,1024]{1,0:T(1,128)S(1)}, f32[1,1024]{1,0:T(1,128)S(1)}, u32[]{:S(2)}, u32[]{:S(2)}) %collective-permute-start.5) | collective-permute-done | bytes 4128 | tf_op jit(solution)/shard_map/ppermute | solution.py:29
  63.5 0.5 collective-permute-done.4.even_found
  64.0 0.6 shard_map.61
Async XLA Ops:
  0.0 8.6 %copy-start = (bf16[3,1024,1024]{2,1,0:T(8,128)(2,1)S(1)}, bf16[3,1024,1024]{2,1,0:T(8,128)(2,1)}, u32[]{:S(2)}) copy-start(bf16[3,1024,1024]{2,1,0:T(8,128)(2,1)} %raw.3) | copy-start | bytes 18874372
  0.0 8.6 %copy-start.1 = (s32[1,6,2]{1,2,0:T(2,128)S(1)}, s32[1,6,2]{1,2,0:T(2,128)}, u32[]{:S(2)}) copy-start(s32[1,6,2]{1,2,0:T(2,128)} %param.8) | copy-start | bytes 148
  1.9 30.4 %collective-permute-start.1 = (bf16[656,1024]{1,0:T(8,128)(2,1)S(1)}, bf16[656,1024]{1,0:T(8,128)(2,1)S(1)}, u32[]{:S(2)}, u32[]{:S(2)}) collective-permute-start(bf16[656,1024]{1,0:T(8,128)(2,1)S(1)} %get-tuple-element.29), channel_id=1, source_target_pairs={{0,1},{2,3},{4,5},{6,7},{8,9},{10,11},{12,13},{14,15},{16,17},{18,... | collective-permute-start | bytes 4030472 | tf_op jit(solution)/shard_map/ppermute | solution.py:29
  3.3 43.3 %collective-permute-start = (bf16[656,1024]{1,0:T(8,128)(2,1)S(1)}, bf16[656,1024]{1,0:T(8,128)(2,1)S(1)}, u32[]{:S(2)}, u32[]{:S(2)}) collective-permute-start(bf16[656,1024]{1,0:T(8,128)(2,1)S(1)} %get-tuple-element.27), channel_id=1, source_target_pairs={{1,2},{3,4},{5,6},{7,8},{9,10},{11,12},{13,14},{15,16},{17,18},{19... | collective-permute-start | bytes 4030472 | tf_op jit(solution)/shard_map/ppermute | solution.py:29
  21.2 31.3 %collective-permute-start.3 = (bf16[384,1024]{1,0:T(8,128)(2,1)S(1)}, bf16[384,1024]{1,0:T(8,128)(2,1)S(1)}, u32[]{:S(2)}, u32[]{:S(2)}) collective-permute-start(bf16[384,1024]{1,0:T(8,128)(2,1)S(1)} %get-tuple-element.37), channel_id=1, source_target_pairs={{0,1},{2,3},{4,5},{6,7},{8,9},{10,11},{12,13},{14,15},{16,17},{18,... | collective-permute-start | bytes 2359304 | tf_op jit(solution)/shard_map/ppermute | solution.py:29
  26.3 28.7 %collective-permute-start.2 = (bf16[384,1024]{1,0:T(8,128)(2,1)S(1)}, bf16[384,1024]{1,0:T(8,128)(2,1)S(1)}, u32[]{:S(2)}, u32[]{:S(2)}) collective-permute-start(bf16[384,1024]{1,0:T(8,128)(2,1)S(1)} %get-tuple-element.33), channel_id=1, source_target_pairs={{1,2},{3,4},{5,6},{7,8},{9,10},{11,12},{13,14},{15,16},{17,18},{19... | collective-permute-start | bytes 2359304 | tf_op jit(solution)/shard_map/ppermute | solution.py:29
  57.4 6.1 %collective-permute-start.5 = (f32[1,1024]{1,0:T(1,128)S(1)}, f32[1,1024]{1,0:T(1,128)S(1)}, u32[]{:S(2)}, u32[]{:S(2)}) collective-permute-start(f32[1,1024]{1,0:T(1,128)S(1)} %get-tuple-element.44), channel_id=1, source_target_pairs={{1,2},{3,4},{5,6},{7,8},{9,10},{11,12},{13,14},{15,16},{17,18},{19... | collective-permute-start | bytes 12296 | tf_op jit(solution)/shard_map/ppermute | solution.py:29
  61.4 2.5 %collective-permute-start.4 = (f32[1,1024]{1,0:T(1,128)S(1)}, f32[1,1024]{1,0:T(1,128)S(1)}, u32[]{:S(2)}, u32[]{:S(2)}) collective-permute-start(f32[1,1024]{1,0:T(1,128)S(1)} %get-tuple-element.43), channel_id=1, source_target_pairs={{0,1},{2,3},{4,5},{6,7},{8,9},{10,11},{12,13},{14,15},{16,17},{18,... | collective-permute-start | bytes 12296 | tf_op jit(solution)/shard_map/ppermute | solution.py:29

commit v3 on v2

--- a/solution.py
+++ b/solution.py
@@ -12,7 +12,8 @@
 HELD = 3
 COLS = 256
 LANES = 128
-NOTE = 16
+GROUPS = DIM // LANES
+NOTE = 4 * GROUPS
 CUTS = ((0, 640, 1024), (0, 640, 1024))
 DIGIT = 128
 DEAD = DIGIT**3 - 1
@@ -53,8 +54,13 @@
 
 def normalize(raw, units, rows):
     def step(index, carry):
-        at = pl.ds(pl.multiple_of(index * LANES, LANES), LANES)
-        units[at, :] = unit_rows(raw[at, :])
+        first = pl.multiple_of(index * LANES, LANES)
+        at = pl.ds(first, LANES)
+        if raw.shape[-1] == DIM:
+            values = raw[at, :]
+        else:
+            values = jnp.concatenate([raw[pl.ds(group * rows + first, LANES), :] for group in range(GROUPS)], axis=1)
+        units[at, :] = unit_rows(values)
         return carry
 
     lax.fori_loop(0, rows // LANES, step, 0, unroll=2 if rows % (2 * LANES) == 0 else True)
@@ -97,25 +103,36 @@
 
 
 def note_rows(keys, flags):
-    row = lax.broadcasted_iota(jnp.int32, (NOTE, ROWS), 0)
-    values = [keys % DIGIT, (keys // DIGIT) % DIGIT, keys // DIGIT**2] + flags
-    note = jnp.zeros((NOTE, ROWS), jnp.int32)
-    for index, value in enumerate(values):
-        note = jnp.where(row == index, value, note)
+    keys = jnp.concatenate([keys[:, group * LANES : (group + 1) * LANES] for group in range(GROUPS)], axis=0)
+    row = lax.broadcasted_iota(jnp.int32, keys.shape, 0)
+    marks = jnp.zeros_like(keys)
+    for index, flag in enumerate(flags):
+        marks = jnp.where(row == index, flag, marks)
+    note = jnp.concatenate([keys % DIGIT, (keys // DIGIT) % DIGIT, keys // DIGIT**2, marks], axis=0)
     return note.astype(jnp.float32).astype(jnp.bfloat16)
 
 
-def noted_keys(note):
+def noted(note):
     digits = note.astype(jnp.float32).astype(jnp.int32)
-    return digits[0:1] + digits[1:2] * DIGIT + digits[2:3] * DIGIT**2
+    low, middle, high, marks = (digits[part * GROUPS : (part + 1) * GROUPS] for part in range(4))
+    keys = low + middle * DIGIT + high * DIGIT**2
+    return jnp.concatenate([keys[group : group + 1] for group in range(GROUPS)], axis=1), marks
 
 
 def piece_copies(items, raw, pieces, sems):
     odd, copies = odd_device(), []
-    for number, ((boundary, index), piece) in enumerate(zip(items, pieces)):
+    for (boundary, index), piece in zip(items, pieces):
         first, rows = CUTS[boundary][index], cut_rows(boundary, index)
         block = (HELD - 1) * (odd if boundary else 1 - odd)
-        copies.append(pltpu.make_async_copy(raw.at[block, pl.ds(first, rows)], piece.at[pl.ds(0, rows)], sems.at[number]))
+        if index == 0:
+            parts = [
+                (raw.at[block, pl.ds(first, rows), pl.ds(group * LANES, LANES)], piece.at[pl.ds(group * rows, rows)])
+                for group in range(GROUPS)
+            ]
+        else:
+            parts = [(raw.at[block, pl.ds(first, rows)], piece)]
+        for source, target in parts:
+            copies.append(pltpu.make_async_copy(source, target, sems.at[len(copies)]))
     return copies
 
 
@@ -151,8 +168,8 @@
     left_flags, right_flags = boundary_flags(pairs)
     note_last = note_rows(keys[HELD - 1 : HELD, :], [])
     note_first = note_rows(keys[0:1, :], right_flags)
-    even_on[pl.ds(cut_rows(0, 0), NOTE), :] = jnp.where(odd == 1, note_first, note_last)
-    odd_on[pl.ds(cut_rows(1, 0), NOTE), :] = jnp.where(odd == 1, note_last, note_first)
+    even_on[pl.ds(cut_rows(0, 0) * GROUPS, NOTE), :] = jnp.where(odd == 1, note_first, note_last)
+    odd_on[pl.ds(cut_rows(1, 0) * GROUPS, NOTE), :] = jnp.where(odd == 1, note_last, note_first)
     for copy in copies:
         copy.wait()
 
@@ -162,7 +179,7 @@
 
 
 def first_pieces(pairs, live, ranks, raw):
-    even, odd = (shaped((cut_rows(boundary, 0) + NOTE, DIM), jnp.bfloat16) for boundary in range(2))
+    even, odd = (shaped((cut_rows(boundary, 0) * GROUPS + NOTE, LANES), jnp.bfloat16) for boundary in range(2))
     return pl.pallas_call(
         first_kernel,
         out_shape=(even, odd, shaped((HELD, ROWS), jnp.int32)),
@@ -172,7 +189,7 @@
             pltpu.SMEM(pairs.shape, jnp.int32),
             pltpu.SMEM(live.shape, jnp.int32),
             pltpu.VMEM(ranks.shape, jnp.int32),
-            pltpu.SemaphoreType.DMA((2,)),
+            pltpu.SemaphoreType.DMA((2 * GROUPS,)),
             pltpu.SemaphoreType.DMA((3,)),
         ],
         compiler_params=pltpu.CompilerParams(vmem_limit_bytes=6 << 20),
@@ -323,11 +340,11 @@
     rows = cut_rows(boundary, 0)
     after = odd_after(boundary)
     right_acc[...] = jnp.full_like(right_acc, NONE)
-    note = raw[pl.ds(rows, NOTE), :]
-    guest_keys[...] = noted_keys(note)
+    noted_keys, marks = noted(raw[pl.ds(rows * GROUPS, NOTE), :])
+    guest_keys[...] = noted_keys
     for which in range(3):
-        noted = (jnp.max(note[3 + which : 4 + which, :].astype(jnp.float32)) > 0.5).astype(jnp.int32)
-        guest_flags[which] = jnp.where(after == 1, noted, flags[which])
+        marked = (jnp.max(marks[which : which + 1, :].astype(jnp.float32)) > 0.5).astype(jnp.int32)
+        guest_flags[which] = jnp.where(after == 1, marked, flags[which])
     guest_pairs(boundary, 0, guest_flags, raw, guest_keys, keys, units, right_acc, *scratch)
     finish_guests(scratch[-1], 0, None, guest_best)
     finish_held(right_acc, best_before, best)

time: 65.3 us -> 65.6 us (level)
  the two profiles are of different devices: /device:TPU:103 before, /device:TPU:1 now
where the time goes in v3:
time: 65.6 us; the launch traced here: 65.1 us
  Pallas kernels  27.8 us (42%)
  waiting for transfers between devices  22.6 us (34%)
  starting transfers between devices  14 us (21%)
  between operations  0.75 us (1%)
    ppermute x6, waiting for transfers between devices, exchanged(): lax.ppermute(value, AXES, pairs + [(high, low) for low, high in pairs])  22.6 us
    ppermute x6, starting transfers between devices, exchanged(): lax.ppermute(value, AXES, pairs + [(high, low) for low, high in pairs])  14 us
    pallas_call x1, Pallas kernels, local_pairs(): pl.pallas_call(local_kernel, out_shape=(shaped((HELD, ROWS, DIM), jnp.bfl...  12.5 us
    pallas_call x2, Pallas kernels, first_guests(): pl.pallas_call(functools.partial(first_guests_kernel, boundary), out_shap...  9.38 us
    pallas_call x2, Pallas kernels, next_guests(): pl.pallas_call(functools.partial(next_guests_kernel, boundary, index), ou...  3.11 us
    pallas_call x1, Pallas kernels, first_pieces(): pl.pallas_call(first_kernel, out_shape=(even, odd, shaped((HELD, ROWS), j...  2.17 us
  transfers between devices with their start and end apart: 6, of which 5 were waited for; matrix products, arithmetic and copies ran while one was open for 0% of the time, Pallas kernels for 35%

profile of v3, /device:TPU:1, one launch (start us, length us, event | category | flops | bytes accessed | tf_op | source)
XLA Modules:
  0.0 65.1 jit_solution(13400696678788533599)
XLA Ops:
  0.0 0.0 copy-start
  0.0 0.0 copy-start.1
  0.0 2.2 %shard_map.55 = (bf16[5152,128]{1,0:T(8,128)(2,1)S(1)}, bf16[5152,128]{1,0:T(8,128)(2,1)S(1)}, s32[3,1024]{1,0:T(4,128)S(1)}) custom-call(s32[1,2,6]{2,1,0:T(2,128)} %bitcast.1, s32[3]{0:T(128)} %live_hbm.1, s32[3,1024]{1,0:T(4,128)} %ranks_hbm.1, bf16[3,1024,1024]{2,1,0:T(8,128)(2,1)} %raw.3), custom_call_target="tpu_custom_call" | custom-call | bytes 4194304 | tf_op jit(solution)/shard_map/pallas_call | solution.py:183
  2.2 2.2 %collective-permute-start.1 = (bf16[5152,128]{1,0:T(8,128)(2,1)S(1)}, bf16[5152,128]{1,0:T(8,128)(2,1)S(1)}, u32[]{:S(2)}, u32[]{:S(2)}) collective-permute-start(bf16[5152,128]{1,0:T(8,128)(2,1)S(1)} %get-tuple-element.29), channel_id=1, source_target_pairs={{0,1},{2,3},{4,5},{6,7},{8,9},{10,11},{12,13},{14,15},{16,17},{18,... | collective-permute-start | bytes 3956744 | tf_op jit(solution)/shard_map/ppermute | solution.py:30
  4.4 4.6 %collective-permute-start = (bf16[5152,128]{1,0:T(8,128)(2,1)S(1)}, bf16[5152,128]{1,0:T(8,128)(2,1)S(1)}, u32[]{:S(2)}, u32[]{:S(2)}) collective-permute-start(bf16[5152,128]{1,0:T(8,128)(2,1)S(1)} %get-tuple-element.27), channel_id=1, source_target_pairs={{1,2},{3,4},{5,6},{7,8},{9,10},{11,12},{13,14},{15,16},{17,18},{19... | collective-permute-start | bytes 3956744 | tf_op jit(solution)/shard_map/ppermute | solution.py:30
  9.7 0.0 copy-done
  9.7 0.0 copy-done.1
  9.7 12.5 %shard_map.56 = (bf16[3,1024,1024]{2,1,0:T(8,128)(2,1)S(1)}, f32[3,1024]{1,0:T(4,128)S(1)}, bf16[384,1024]{1,0:T(8,128)(2,1)S(1)}, bf16[384,1024]{1,0:T(8,128)(2,1)S(1)}, s32[3]{0:T(128)S(1)}) custom-call(s32[1,2,6]{2,1,0:T(2,128)S(1)} %bitcast.2, s32[1]{0:T(128)S(6)} %copy.6.count, bf16[3,1024,1024]{2,1,0:T(8,128)(2,1)S(1)} %copy-done, ...), custom_call_target="tpu_custom_call" | custom-call | flops 2147483648 | bytes 12582912 | tf_op jit(solution)/shard_map/pallas_call | solution.py:250
  22.3 0.1 collective-permute-start.3
  22.4 1.9 %collective-permute-start.2 = (bf16[384,1024]{1,0:T(8,128)(2,1)S(1)}, bf16[384,1024]{1,0:T(8,128)(2,1)S(1)}, u32[]{:S(2)}, u32[]{:S(2)}) collective-permute-start(bf16[384,1024]{1,0:T(8,128)(2,1)S(1)} %get-tuple-element.33), channel_id=1, source_target_pairs={{1,2},{3,4},{5,6},{7,8},{9,10},{11,12},{13,14},{15,16},{17,18},{19... | collective-permute-start | bytes 2359304 | tf_op jit(solution)/shard_map/ppermute | solution.py:30
  24.3 7.5 %collective-permute-done.1.raw = bf16[5152,128]{1,0:T(8,128)(2,1)S(1)} collective-permute-done((bf16[5152,128]{1,0:T(8,128)(2,1)S(1)}, bf16[5152,128]{1,0:T(8,128)(2,1)S(1)}, u32[]{:S(2)}, u32[]{:S(2)}) %collective-permute-start.1) | collective-permute-done | bytes 1318944 | tf_op jit(solution)/shard_map/ppermute | solution.py:30
  31.8 3.6 %shard_map.57 = (f32[1,640]{1,0:T(1,128)S(1)}, f32[3,1024]{1,0:T(4,128)S(1)}, s32[1,1024]{1,0:T(1,128)S(1)}, s32[3]{0:T(128)S(1)}) custom-call(s32[3]{0:T(128)S(1)} %get-tuple-element.26.flags, bf16[5152,128]{1,0:T(8,128)(2,1)S(1)} %collective-permute-done.1.raw, s32[3,1024]{1,0:T(4,128)S(1)} %get-tuple-element.25.keys, ...), custom_call_target="tpu_custom_call" | custom-call | flops 1342177280 | bytes 7602176 | tf_op jit(solution)/shard_map/pallas_call | solution.py:355
  35.5 10.8 %collective-permute-done.raw = bf16[5152,128]{1,0:T(8,128)(2,1)S(1)} collective-permute-done((bf16[5152,128]{1,0:T(8,128)(2,1)S(1)}, bf16[5152,128]{1,0:T(8,128)(2,1)S(1)}, u32[]{:S(2)}, u32[]{:S(2)}) %collective-permute-start) | collective-permute-done | bytes 1318944 | tf_op jit(solution)/shard_map/ppermute | solution.py:30
  46.2 5.8 %shard_map.58 = (f32[1,640]{1,0:T(1,128)S(1)}, f32[3,1024]{1,0:T(4,128)S(1)}, s32[1,1024]{1,0:T(1,128)S(1)}, s32[3]{0:T(128)S(1)}) custom-call(s32[3]{0:T(128)S(1)} %get-tuple-element.26.flags, bf16[5152,128]{1,0:T(8,128)(2,1)S(1)} %collective-permute-done.raw, s32[3,1024]{1,0:T(4,128)S(1)} %get-tuple-element.25.keys, ...), custom_call_target="tpu_custom_call" | custom-call | flops 1342177280 | bytes 7602176 | tf_op jit(solution)/shard_map/pallas_call | solution.py:355
  52.0 0.0 collective-permute-done.3.raw
  52.0 0.8 %shard_map.59 = (f32[1,1024]{1,0:T(1,128)S(1)}, f32[3,1024]{1,0:T(4,128)S(1)}) custom-call(s32[3]{0:T(128)S(1)} %get-tuple-element.36.flags, bf16[384,1024]{1,0:T(8,128)(2,1)S(1)} %collective-permute-done.3.raw, s32[1,1024]{1,0:T(1,128)S(1)} %get-tuple-element.38.guest_keys, f32[1,640]{1,0:T(1,128)S(1)} %get-tuple-element.39.guest_earlier, ...), custom_call_target="tpu_custom_call" | custom-call | flops 805306368 | bytes 7077888 | tf_op jit(solution)/shard_map/pallas_call | solution.py:382
  52.8 1.8 %collective-permute-done.2.raw = bf16[384,1024]{1,0:T(8,128)(2,1)S(1)} collective-permute-done((bf16[384,1024]{1,0:T(8,128)(2,1)S(1)}, bf16[384,1024]{1,0:T(8,128)(2,1)S(1)}, u32[]{:S(2)}, u32[]{:S(2)}) %collective-permute-start.2) | collective-permute-done | bytes 786464 | tf_op jit(solution)/shard_map/ppermute | solution.py:30
  54.6 2.3 %shard_map.60 = (f32[1,1024]{1,0:T(1,128)S(1)}, f32[3,1024]{1,0:T(4,128)S(1)}) custom-call(s32[3]{0:T(128)S(1)} %get-tuple-element.32.flags, bf16[384,1024]{1,0:T(8,128)(2,1)S(1)} %collective-permute-done.2.raw, s32[1,1024]{1,0:T(1,128)S(1)} %get-tuple-element.34.guest_keys, f32[1,640]{1,0:T(1,128)S(1)} %get-tuple-element.35.guest_earlier, ...), custom_call_target="tpu_custom_call" | custom-call | flops 805306368 | bytes 7077888 | tf_op jit(solution)/shard_map/pallas_call | solution.py:382
  56.9 5.0 %collective-permute-start.5 = (f32[1,1024]{1,0:T(1,128)S(1)}, f32[1,1024]{1,0:T(1,128)S(1)}, u32[]{:S(2)}, u32[]{:S(2)}) collective-permute-start(f32[1,1024]{1,0:T(1,128)S(1)} %get-tuple-element.44), channel_id=1, source_target_pairs={{1,2},{3,4},{5,6},{7,8},{9,10},{11,12},{13,14},{15,16},{17,18},{19... | collective-permute-start | bytes 12296 | tf_op jit(solution)/shard_map/ppermute | solution.py:30
  62.0 0.1 collective-permute-start.4
  62.1 1.2 %collective-permute-done.5.odd_found = f32[1,1024]{1,0:T(1,128)S(1)} collective-permute-done((f32[1,1024]{1,0:T(1,128)S(1)}, f32[1,1024]{1,0:T(1,128)S(1)}, u32[]{:S(2)}, u32[]{:S(2)}) %collective-permute-start.5) | collective-permute-done | bytes 4128 | tf_op jit(solution)/shard_map/ppermute | solution.py:30
  63.2 1.3 %collective-permute-done.4.even_found = f32[1,1024]{1,0:T(1,128)S(1)} collective-permute-done((f32[1,1024]{1,0:T(1,128)S(1)}, f32[1,1024]{1,0:T(1,128)S(1)}, u32[]{:S(2)}, u32[]{:S(2)}) %collective-permute-start.4) | collective-permute-done | bytes 4128 | tf_op jit(solution)/shard_map/ppermute | solution.py:30
  64.5 0.6 shard_map.61
Async XLA Ops:
  0.0 9.7 %copy-start = (bf16[3,1024,1024]{2,1,0:T(8,128)(2,1)S(1)}, bf16[3,1024,1024]{2,1,0:T(8,128)(2,1)}, u32[]{:S(2)}) copy-start(bf16[3,1024,1024]{2,1,0:T(8,128)(2,1)} %raw.3) | copy-start | bytes 18874372
  0.0 9.7 %copy-start.1 = (s32[1,6,2]{1,2,0:T(2,128)S(1)}, s32[1,6,2]{1,2,0:T(2,128)}, u32[]{:S(2)}) copy-start(s32[1,6,2]{1,2,0:T(2,128)} %param.8) | copy-start | bytes 148
  2.2 29.6 %collective-permute-start.1 = (bf16[5152,128]{1,0:T(8,128)(2,1)S(1)}, bf16[5152,128]{1,0:T(8,128)(2,1)S(1)}, u32[]{:S(2)}, u32[]{:S(2)}) collective-permute-start(bf16[5152,128]{1,0:T(8,128)(2,1)S(1)} %get-tuple-element.29), channel_id=1, source_target_pairs={{0,1},{2,3},{4,5},{6,7},{8,9},{10,11},{12,13},{14,15},{16,17},{18,... | collective-permute-start | bytes 3956744 | tf_op jit(solution)/shard_map/ppermute | solution.py:30
  4.4 41.8 %collective-permute-start = (bf16[5152,128]{1,0:T(8,128)(2,1)S(1)}, bf16[5152,128]{1,0:T(8,128)(2,1)S(1)}, u32[]{:S(2)}, u32[]{:S(2)}) collective-permute-start(bf16[5152,128]{1,0:T(8,128)(2,1)S(1)} %get-tuple-element.27), channel_id=1, source_target_pairs={{1,2},{3,4},{5,6},{7,8},{9,10},{11,12},{13,14},{15,16},{17,18},{19... | collective-permute-start | bytes 3956744 | tf_op jit(solution)/shard_map/ppermute | solution.py:30
  22.3 29.7 %collective-permute-start.3 = (bf16[384,1024]{1,0:T(8,128)(2,1)S(1)}, bf16[384,1024]{1,0:T(8,128)(2,1)S(1)}, u32[]{:S(2)}, u32[]{:S(2)}) collective-permute-start(bf16[384,1024]{1,0:T(8,128)(2,1)S(1)} %get-tuple-element.37), channel_id=1, source_target_pairs={{0,1},{2,3},{4,5},{6,7},{8,9},{10,11},{12,13},{14,15},{16,17},{18,... | collective-permute-start | bytes 2359304 | tf_op jit(solution)/shard_map/ppermute | solution.py:30
  22.4 32.3 %collective-permute-start.2 = (bf16[384,1024]{1,0:T(8,128)(2,1)S(1)}, bf16[384,1024]{1,0:T(8,128)(2,1)S(1)}, u32[]{:S(2)}, u32[]{:S(2)}) collective-permute-start(bf16[384,1024]{1,0:T(8,128)(2,1)S(1)} %get-tuple-element.33), channel_id=1, source_target_pairs={{1,2},{3,4},{5,6},{7,8},{9,10},{11,12},{13,14},{15,16},{17,18},{19... | collective-permute-start | bytes 2359304 | tf_op jit(solution)/shard_map/ppermute | solution.py:30
  56.9 6.3 %collective-permute-start.5 = (f32[1,1024]{1,0:T(1,128)S(1)}, f32[1,1024]{1,0:T(1,128)S(1)}, u32[]{:S(2)}, u32[]{:S(2)}) collective-permute-start(f32[1,1024]{1,0:T(1,128)S(1)} %get-tuple-element.44), channel_id=1, source_target_pairs={{1,2},{3,4},{5,6},{7,8},{9,10},{11,12},{13,14},{15,16},{17,18},{19... | collective-permute-start | bytes 12296 | tf_op jit(solution)/shard_map/ppermute | solution.py:30
  62.0 2.5 %collective-permute-start.4 = (f32[1,1024]{1,0:T(1,128)S(1)}, f32[1,1024]{1,0:T(1,128)S(1)}, u32[]{:S(2)}, u32[]{:S(2)}) collective-permute-start(f32[1,1024]{1,0:T(1,128)S(1)} %get-tuple-element.43), channel_id=1, source_target_pairs={{0,1},{2,3},{4,5},{6,7},{8,9},{10,11},{12,13},{14,15},{16,17},{18,... | collective-permute-start | bytes 12296 | tf_op jit(solution)/shard_map/ppermute | solution.py:30
